TPU v7x, 256 devices: a whole 4x4x8 slice. The times are simulated.
256 devices in a mesh: tm: 16 (over z, core), head: 16 (over y, x).
Axes of the slice: x: 4, y: 4, z: 8, core: 2. Of those that a mesh axis runs over, the one named last changes fastest.
Arguments:
- start: float32 [2048, 64], P('head'), may hold values from -6 to 6
- latents: float32 [16, 2048, 64], P('tm', 'head'), may hold values from -12 to 12
- time_mod: float32 [16, 3, 3072], P('tm'), may hold values from -3 to 3
- steps_window: int32 [16], P('tm'), may hold values from 0 to 999
- ddim_table: float32 [1000, 2], replicated, may hold values from -0.5 to 0.5
- w_in: bfloat16 [64, 3072], replicated, may hold values from -0.75 to 0.75
- w_qkv: bfloat16 [3, 3072, 3072], P(None, 'head'), may hold values from -0.28867513 to 0.28867513
- w_attn_out: bfloat16 [3072, 3072], P('head'), may hold values from -0.109375 to 0.109375
- w_proj: bfloat16 [3072, 64], replicated, may hold values from -0.109375 to 0.109375
Outputs:
- refreshed: float32 [16, 2048, 64], P('tm', 'head')
- worst_error: float32 [], replicated
All inputs are finite; a program needn't handle non-finite values.
Results may differ from a plain program's by a relative error of at most 0.0031.
Values may be sent and summed in bfloat16 or wider, within the bound.
No kernel may reach another device: no remote copies, remote signals or barrier semaphores. Data moves between devices by JAX's collectives and lax.ppermute only.
A program may use at most 128 MiB of HBM per device.

v0:
```python
import jax
import jax.numpy as jnp
from jax import lax
from jax.sharding import PartitionSpec as P

HD = 64


def passed_along(x, axis, by):
    devices = lax.axis_size(axis)
    pairs = [(i, i + by) for i in range(devices) if 0 <= i + by < devices]
    return lax.ppermute(x, axis, pairs)


def entering(x, axis, combine, identity):
    devices, position = (lax.axis_size(axis), lax.axis_index(axis))
    everything = lax.all_gather(x, axis)
    start = jnp.broadcast_to(jnp.asarray(identity, x.dtype), x.shape)

    def step(k, before):
        reached = k < position
        new = combine(before, everything[k])
        return jnp.where(reached, new, before)

    return lax.fori_loop(0, devices, step, start)


def layer_norm(values_in):
    average = jnp.mean(values_in, -1, keepdims=True)
    centred = values_in - average
    variance = jnp.mean(centred * centred, -1, keepdims=True)
    return centred * lax.rsqrt(variance + 1e-05)


def add_pair(earlier, later):
    return earlier + later


def on_device(start, latents, time_mod, steps_window, ddim_table, w_in, w_qkv, w_attn_out, w_proj):
    position = lax.axis_index("tm")
    behind = passed_along(latents, "tm", 1)
    current = jnp.where(position == 0, start, behind[0])
    rounded = current.astype(jnp.bfloat16)
    hidden = jnp.dot(rounded, w_in, preferred_element_type=jnp.float32)
    shift_mod = time_mod[0, 0]
    scale_mod = time_mod[0, 1]
    gate_mod = time_mod[0, 2]
    embedded = jnp.dot(
        lax.all_gather(rounded, "head", axis=0, tiled=True),
        w_in,
        preferred_element_type=jnp.float32,
    )
    normed = (layer_norm(embedded) * (1.0 + scale_mod) + shift_mod).astype(jnp.bfloat16)
    stacked = jnp.einsum("rd,ckd->crk", normed, w_qkv, preferred_element_type=jnp.float32).astype(
        jnp.bfloat16
    )
    seq_len = stacked.shape[1]
    local_heads = w_qkv.shape[1] // HD
    per_head = stacked.reshape(3, seq_len, local_heads, HD)
    span_rows = 512

    def attend_block(block_id):
        queries = lax.dynamic_slice_in_dim(per_head[0], block_id * span_rows, span_rows, 0)
        scores = jnp.einsum(
            "qhd,khd->hqk", queries, per_head[1], preferred_element_type=jnp.float32
        ) * HD ** (-0.5)
        weights = jax.nn.softmax(scores, -1).astype(jnp.bfloat16)
        return jnp.einsum(
            "hqk,khd->qhd", weights, per_head[2], preferred_element_type=jnp.float32
        ).astype(jnp.bfloat16)

    attended = lax.map(attend_block, jnp.arange(seq_len // span_rows, dtype=jnp.int32))
    attended = attended.reshape(seq_len, local_heads * HD)
    own_rows = current.shape[0]
    projected = lax.psum_scatter(
        jnp.dot(attended, w_attn_out, preferred_element_type=jnp.float32),
        "head",
        scatter_dimension=0,
        tiled=True,
    )
    residual_sum = hidden + gate_mod * projected
    predicted = jnp.dot(
        residual_sum.astype(jnp.bfloat16), w_proj, preferred_element_type=jnp.float32
    )
    one_hot = (steps_window[0] == jnp.arange(ddim_table.shape[0], dtype=jnp.int32)).astype(
        jnp.float32
    )
    coefs_row = jnp.dot(one_hot, ddim_table, precision=lax.Precision.HIGHEST)
    drift_term = coefs_row[0] * current + coefs_row[1] * predicted
    earlier_sum = entering(drift_term, "tm", add_pair, jnp.zeros_like(drift_term))
    refreshed = start + earlier_sum + drift_term
    difference = refreshed - latents[0]
    own_error = jnp.sum(difference * difference)
    summed = lax.psum(own_error, "head")
    largest = lax.pmax(summed, "tm")
    cells = own_rows * lax.axis_size("head") * current.shape[1]
    return (refreshed[None], largest / cells)


def solution(mesh):
    in_specs = (
        P("head", None),
        P("tm", "head", None),
        P("tm", None, None),
        P("tm"),
        P(),
        P(),
        P(None, "head", None),
        P("head", None),
        P(),
    )
    out_specs = (P("tm", "head", None), P())
    return jax.shard_map(
        on_device, mesh=mesh, in_specs=in_specs, out_specs=out_specs, check_vma=False
    )
```

profile of v0, /device:TPU:1, one launch (start us, length us, event | category | flops | bytes accessed | tf_op | source)
XLA Modules:
  0.0 443.7 jit_solution(1954543078828721929)
XLA Ops:
  7.2 5.2 %collective-permute-start = (f32[1,128,64]{1,2,0:T(8,128)}, f32[1,128,64]{1,2,0:T(8,128)}, u32[]{:S(2)}, u32[]{:S(2)}) collective-permute-start(f32[1,128,64]{1,2,0:T(8,128)} %param.14), channel_id=1, source_target_pairs={{0,16},{16,32},{32,48},{48,64},{64,80},{80,96},{96,112},{112,128},... | collective-permute-start | bytes 98312 | tf_op jit(solution)/shard_map/ppermute | solution.py:12
  14.6 20.9 %all_gather.9 = bf16[2048,64]{0,1:T(8,128)(2,1)} all-gather(bf16[128,64]{0,1:T(8,128)(2,1)S(1)} %fusion.49), channel_id=1, replica_groups=mesh['tm'=16,'head'=16] {'head'}, dimensions={0}, use_global_device_ids=true | all-gather | bytes 278528 | tf_op jit(solution)/shard_map/all_gather | solution.py:49
  35.5 4.6 %fusion.64 = (f32[2048]{0:T(1024)S(1)}, f32[2048,3072]{1,0:T(8,128)S(1)}) fusion(bf16[2048,64]{0,1:T(8,128)(2,1)} %all_gather.9, bf16[64,3072]{1,0:T(8,128)(2,1)} %param.18), kind=kOutput, calls=%fused_computation.52 | convolution fusion | flops 811595776 | bytes 25829376 | tf_op jit(solution)/shard_map/dot_general | solution.py:48
  40.2 3.6 multiply_reduce_fusion.1
  43.7 4.7 %copy-done.2 = f32[2048,3072]{1,0:T(8,128)} copy-done((f32[2048,3072]{1,0:T(8,128)}, f32[2048,3072]{1,0:T(8,128)S(1)}, u32[]{:S(2)}) %copy-start.2) | copy-done | bytes 25165848
  48.5 13.8 %fusion.41 = bf16[2048,3,192]{0,2,1:T(8,128)(2,1)} fusion(bf16[3,192,3072]{2,1,0:T(8,128)(2,1)S(1)} %copy-done, f32[2048,3072]{1,0:T(8,128)} %copy-done.2, f32[3072]{0:T(1024)S(1)} %bitcast.101, f32[3072]{0:T(1024)S(1)} %bitcast.102, f32[2048]{0:T(1024)S(1)} %add_rsqrt_fusion, f32[2048]{0:T(1024)S(1)} %broadcast_multiply_fusion), kind=kOutput, calls=%fused_computation.32 | convolution fusion | flops 7280394240 | bytes 31105024 | tf_op jit(solution)/shard_map/rd,ckd->crk/dot_general | solution.py:54
  62.3 76.9 %while.24 = (s32[]{:T(128)}, bf16[4,512,3,64]{1,3,2,0:T(8,128)(2,1)}, bf16[3,2048,3,64]{1,3,2,0:T(8,128)(2,1)}, s32[4]{0:T(128)S(1)}, s32[]{:T(128)}, /*index=5*/s32[1]{0:T(128)}, s32[]{:T(128)}, s32[]{:T(128)}) while((s32[]{:T(128)}, bf16[4,512,3,64]{1,3,2,0:T(8,128)(2,1)}, bf16[3,2048,3,64]{1,3,2,0:T(8,128)(2,1)}, s32[4]{0:T(128)S(1)}, ...), condition=%wide.region_5.6_spmd, body=%wide.region_2.5_spmd.sunk | while | flops 821135360 | bytes 28717716 | solution.py:72
  64.7 9.3 %fusion.83 = (f32[3,512]{1,0:T(4,128)S(1)}, f32[3,512,2048]{2,1,0:T(8,128)}) fusion(bf16[3,2048,3,64]{1,3,2,0:T(8,128)(2,1)} %get-tuple-element.227, bf16[1,2048,3,64]{1,3,2,0:T(8,128)(2,1)S(1)} %slice.59, s32[]{:T(128)S(6)} %select_n.53), kind=kOutput, calls=%fused_computation.49.clone.1 | convolution fusion | flops 412092416 | bytes 13572100 | tf_op jit(solution)/shard_map/while/body/eval_jaxpr/sub | solution.py:67
  74.0 7.5 %fusion.84 = bf16[4,512,3,64]{1,3,2,0:T(8,128)(2,1)} fusion(bf16[4,512,3,64]{1,3,2,0:T(8,128)(2,1)} %get-tuple-element.218, s32[]{:T(128)} %get-tuple-element.217, f32[3,512,2048]{2,1,0:T(8,128)} %get-tuple-element.203, f32[3,512]{1,0:T(4,128)S(1)} %get-tuple-element.204, bf16[3,2048,3,64]{1,3,2,0:T(8,128)(2,1)} %get-tuple-element.227), kind=kOutput, calls=%fused_computation.10.clone.1 | convolution fusion | flops 409042944 | bytes 13572608 | tf_op jit(solution)/shard_map/while/body/eval_jaxpr/hqk,khd->qhd/dot_general | solution.py:68
  84.0 9.3 %fusion.83 = (f32[3,512]{1,0:T(4,128)S(1)}, f32[3,512,2048]{2,1,0:T(8,128)}) fusion(bf16[3,2048,3,64]{1,3,2,0:T(8,128)(2,1)} %get-tuple-element.227, bf16[1,2048,3,64]{1,3,2,0:T(8,128)(2,1)S(1)} %slice.59, s32[]{:T(128)S(6)} %select_n.53), kind=kOutput, calls=%fused_computation.49.clone.1 | convolution fusion | flops 412092416 | bytes 13572100 | tf_op jit(solution)/shard_map/while/body/eval_jaxpr/sub | solution.py:67
  93.3 7.5 %fusion.84 = bf16[4,512,3,64]{1,3,2,0:T(8,128)(2,1)} fusion(bf16[4,512,3,64]{1,3,2,0:T(8,128)(2,1)} %get-tuple-element.218, s32[]{:T(128)} %get-tuple-element.217, f32[3,512,2048]{2,1,0:T(8,128)} %get-tuple-element.203, f32[3,512]{1,0:T(4,128)S(1)} %get-tuple-element.204, bf16[3,2048,3,64]{1,3,2,0:T(8,128)(2,1)} %get-tuple-element.227), kind=kOutput, calls=%fused_computation.10.clone.1 | convolution fusion | flops 409042944 | bytes 13572608 | tf_op jit(solution)/shard_map/while/body/eval_jaxpr/hqk,khd->qhd/dot_general | solution.py:68
  103.2 9.3 %fusion.83 = (f32[3,512]{1,0:T(4,128)S(1)}, f32[3,512,2048]{2,1,0:T(8,128)}) fusion(bf16[3,2048,3,64]{1,3,2,0:T(8,128)(2,1)} %get-tuple-element.227, bf16[1,2048,3,64]{1,3,2,0:T(8,128)(2,1)S(1)} %slice.59, s32[]{:T(128)S(6)} %select_n.53), kind=kOutput, calls=%fused_computation.49.clone.1 | convolution fusion | flops 412092416 | bytes 13572100 | tf_op jit(solution)/shard_map/while/body/eval_jaxpr/sub | solution.py:67
  112.5 7.5 %fusion.84 = bf16[4,512,3,64]{1,3,2,0:T(8,128)(2,1)} fusion(bf16[4,512,3,64]{1,3,2,0:T(8,128)(2,1)} %get-tuple-element.218, s32[]{:T(128)} %get-tuple-element.217, f32[3,512,2048]{2,1,0:T(8,128)} %get-tuple-element.203, f32[3,512]{1,0:T(4,128)S(1)} %get-tuple-element.204, bf16[3,2048,3,64]{1,3,2,0:T(8,128)(2,1)} %get-tuple-element.227), kind=kOutput, calls=%fused_computation.10.clone.1 | convolution fusion | flops 409042944 | bytes 13572608 | tf_op jit(solution)/shard_map/while/body/eval_jaxpr/hqk,khd->qhd/dot_general | solution.py:68
  122.4 9.3 %fusion.83 = (f32[3,512]{1,0:T(4,128)S(1)}, f32[3,512,2048]{2,1,0:T(8,128)}) fusion(bf16[3,2048,3,64]{1,3,2,0:T(8,128)(2,1)} %get-tuple-element.227, bf16[1,2048,3,64]{1,3,2,0:T(8,128)(2,1)S(1)} %slice.59, s32[]{:T(128)S(6)} %select_n.53), kind=kOutput, calls=%fused_computation.49.clone.1 | convolution fusion | flops 412092416 | bytes 13572100 | tf_op jit(solution)/shard_map/while/body/eval_jaxpr/sub | solution.py:67
  131.7 7.5 %fusion.84 = bf16[4,512,3,64]{1,3,2,0:T(8,128)(2,1)} fusion(bf16[4,512,3,64]{1,3,2,0:T(8,128)(2,1)} %get-tuple-element.218, s32[]{:T(128)} %get-tuple-element.217, f32[3,512,2048]{2,1,0:T(8,128)} %get-tuple-element.203, f32[3,512]{1,0:T(4,128)S(1)} %get-tuple-element.204, bf16[3,2048,3,64]{1,3,2,0:T(8,128)(2,1)} %get-tuple-element.227), kind=kOutput, calls=%fused_computation.10.clone.1 | convolution fusion | flops 409042944 | bytes 13572608 | tf_op jit(solution)/shard_map/while/body/eval_jaxpr/hqk,khd->qhd/dot_general | solution.py:68
  139.2 1.7 copy.13
  141.1 10.1 %fusion.65 = f32[2048,3072]{1,0:T(8,128)} fusion(bf16[2048,192]{0,1:T(8,128)(2,1)S(1)} %bitcast.97, bf16[192,3072]{1,0:T(8,128)(2,1)S(1)} %copy-done.3), kind=kOutput, calls=%fused_computation.53 | convolution fusion | flops 2415919104 | bytes 27131904 | tf_op jit(solution)/shard_map/dot_general | solution.py:76
  153.8 163.4 %reduce-scatter.2.cloned.1.call-done = f32[128,3072]{1,0:T(8,128)} async-done(((f32[2048,3072]{1,0:T(8,128)}), f32[128,3072]{1,0:T(8,128)}) %reduce-scatter.2.cloned.1.call-update) | async-done | bytes 1572880 | tf_op jit(solution)/shard_map/reduce_scatter | solution.py:75
  317.2 4.3 multiply_add_fusion
  321.6 20.9 %all-gather = f32[2048,64]{0,1:T(8,128)} all-gather(f32[128,64]{0,1:T(8,128)} %multiply_add_fusion), channel_id=2, replica_groups=mesh['tm'=16,'head'=16] {'tm'}, dimensions={0}, use_global_device_ids=true | all-gather | bytes 557056 | tf_op jit(solution)/shard_map/all_gather | solution.py:17
  342.5 2.4 copy.16
  344.9 23.9 %while.25 = (s32[]{:T(128)}, f32[128,64]{1,0:T(8,128)}, s32[]{:T(128)}, f32[16,128,64]{2,1,0:T(8,128)}, s32[]{:T(128)}, /*index=5*/s32[]{:T(128)}) while((s32[]{:T(128)}, f32[128,64]{1,0:T(8,128)}, s32[]{:T(128)}, f32[16,128,64]{2,1,0:T(8,128)}, s32[]{:T(128)}, /*index=5*/s32[]{:T(128)}) %tuple.68), condition=%wide.region_8.9_spmd.clone, body=%wide.region_7.8_spmd.clone.sunk | while | flops 24580 | bytes 98397 | solution.py:25
  346.3 1.5 add_select_fusion.2
  347.8 1.5 add_select_fusion.2
  352.3 1.5 add_select_fusion.2
  353.8 1.5 add_select_fusion.2
  355.3 1.5 add_select_fusion.2
  356.8 1.5 add_select_fusion.2
  368.8 1.5 copy.15
  370.3 2.0 fusion.48
  372.3 31.8 %psum.7 = f32[]{:T(128)} all-reduce(f32[]{:T(128)} %get-tuple-element.146), channel_id=1, replica_groups=mesh['tm'=16,'head'=16] {'head'}, use_global_device_ids=true, to_apply=%region_10.11 | all-reduce | flops 1 | bytes 8 | tf_op jit(solution)/shard_map/psum | solution.py:94
  404.2 30.9 %pmax.7 = f32[]{:T(128)} all-reduce(f32[]{:T(128)} %psum.7), channel_id=1, replica_groups=mesh['tm'=16,'head'=16] {'tm'}, use_global_device_ids=true, to_apply=%region_11.12 | all-reduce | flops 1 | bytes 8 | tf_op jit(solution)/shard_map/pmax | solution.py:95
  (44 shorter events, 26.2 us)
Async XLA Ops:
  7.2 41.3 %copy-start = (bf16[3,192,3072]{2,1,0:T(8,128)(2,1)S(1)}, bf16[3,192,3072]{2,1,0:T(8,128)(2,1)}, u32[]{:S(2)}) copy-start(bf16[3,192,3072]{2,1,0:T(8,128)(2,1)} %param.19) | copy-start | bytes 10616836
  7.2 310.0 %reduce-scatter.2.cloned.1.call-start = ((), (), s32[]{:S(2)}) async-start(), calls=%async_computation.1 | async-start | bytes 26738688 | tf_op jit(solution)/shard_map/reduce_scatter | solution.py:75
  7.2 6.6 %collective-permute-start = (f32[1,128,64]{1,2,0:T(8,128)}, f32[1,128,64]{1,2,0:T(8,128)}, u32[]{:S(2)}, u32[]{:S(2)}) collective-permute-start(f32[1,128,64]{1,2,0:T(8,128)} %param.14), channel_id=1, source_target_pairs={{0,16},{16,32},{32,48},{48,64},{64,80},{80,96},{96,112},{112,128},... | collective-permute-start | bytes 98312 | tf_op jit(solution)/shard_map/ppermute | solution.py:12
  40.1 8.3 %copy-start.2 = (f32[2048,3072]{1,0:T(8,128)}, f32[2048,3072]{1,0:T(8,128)S(1)}, u32[]{:S(2)}) copy-start(f32[2048,3072]{1,0:T(8,128)S(1)} %get-tuple-element.154) | copy-start | bytes 75497472
  40.1 8.3 %copy-start.4 = (f32[1,1,3072]{2,0,1:T(1,128)S(1)}, f32[1,1,3072]{2,0,1:T(1,128)}, u32[]{:S(2)}) copy-start(f32[1,1,3072]{2,0,1:T(1,128)} %get-tuple-element.149) | copy-start | bytes 36868
  40.2 8.3 %copy-start.5 = (f32[1,1,3072]{2,0,1:T(1,128)S(1)}, f32[1,1,3072]{2,0,1:T(1,128)}, u32[]{:S(2)}) copy-start(f32[1,1,3072]{2,0,1:T(1,128)} %get-tuple-element.150) | copy-start | bytes 36868
  62.3 78.9 %copy-start.3 = (bf16[192,3072]{1,0:T(8,128)(2,1)S(1)}, bf16[192,3072]{1,0:T(8,128)(2,1)}, u32[]{:S(2)}) copy-start(bf16[192,3072]{1,0:T(8,128)(2,1)} %param.20) | copy-start | bytes 3538948
  151.3 284.4 %copy-start.1 = (bf16[3,192,3072]{2,1,0:T(8,128)(2,1)S(1)}, bf16[3,192,3072]{2,1,0:T(8,128)(2,1)}, u32[]{:S(2)}) copy-start(bf16[3,192,3072]{2,1,0:T(8,128)(2,1)} %param.19) | copy-start | bytes 10616836
Sparse Core Ops, SparseCore 0:
  151.4 165.7 reduce-scatter.1
where the time goes:
time: 445 us; the launch traced here: 444 us
  waiting for transfers between devices  163 us (37%)
  blocking collectives  105 us (24%)
  matrix products  101 us (23%)
  other arithmetic  31.6 us (7%)
  local copies, waits for them, and re-layouts  18.4 us (4%)
  between operations  16.7 us (4%)
  starting transfers between devices  5.24 us (1%)
    reduce_scatter x1, waiting for transfers between devices, on_device(): lax.psum_scatter(jnp.dot(attended, w_attn_out, preferred_element_type=jnp...  163 us
    sub x4, matrix products, attend_block(): weights = jax.nn.softmax(scores, -1).astype(jnp.bfloat16)  37.2 us
    psum x1, blocking collectives, on_device(): summed = lax.psum(own_error, 'head')  31.8 us
    pmax x1, blocking collectives, on_device(): largest = lax.pmax(summed, 'tm')  30.9 us
    dot_general x4, matrix products, attend_block(): jnp.einsum('hqk,khd->qhd', weights, per_head[2], preferred_element_type=j...  29.9 us
    select_n x16, other arithmetic, step(): return jnp.where(reached, new, before)  23.9 us
    all_gather x1, blocking collectives, entering(): everything = lax.all_gather(x, axis)  20.9 us
    all_gather x1, blocking collectives, on_device(): lax.all_gather(rounded, 'head', axis=0, tiled=True)  20.9 us
  transfers between devices with their start and end apart: 2, of which 1 were waited for; matrix products, arithmetic and copies ran while one was open for 1% of the time, Pallas kernels for 0%

commit v1 on v0

v1 whole, which is shorter than its diff:
```python
import functools

import jax
import jax.numpy as jnp
from jax import lax
from jax.experimental import pallas as pl
from jax.experimental.pallas import tpu as pltpu
from jax.sharding import PartitionSpec as P

HD = 64
LANES = 128
LOG2E = 1.4426950408889634
SAFE = 100.0
F32 = jnp.float32
BF16 = jnp.bfloat16
NT = (((1,), (1,)), ((), ()))
MIB = 1 << 20


def lane_ids(shape):
    return lax.broadcasted_iota(jnp.int32, shape, len(shape) - 1)


def row_ids(shape):
    return lax.broadcasted_iota(jnp.int32, shape, 0)


def exact_dot(a, b):
    return jnp.dot(a, b, precision=lax.Precision.HIGHEST, preferred_element_type=F32)


def split_rows(values, before, after):
    head = values.astype(BF16)
    rest = (values - head.astype(F32)).astype(BF16)
    width = values.shape[1]
    parts = []
    for part in (head, rest):
        if before:
            parts.append(jnp.zeros((before, width), BF16))
        parts.append(part)
        if after:
            parts.append(jnp.zeros((after, width), BF16))
    return jnp.concatenate(parts, 0)


def weights_kernel(
    steps_ref, mod_ref, w_in_ref, w_qkv_ref, w_out_ref, w_proj_ref, lat_ref, table_ref,
    params_ref, w_io_ref, lat_pay_ref, coefs_ref, proj_sum, out_sum, io_sum, average,
):
    k = pl.program_id(0)
    local_heads = w_qkv_ref.shape[1] // HD
    cols = w_qkv_ref.shape[2]

    @pl.when(k == 0)
    def _():
        proj_sum[...] = jnp.zeros_like(proj_sum)
        out_sum[...] = jnp.zeros_like(out_sum)
        io_sum[...] = jnp.zeros_like(io_sum)
        average[...] = jnp.mean(w_in_ref[...].astype(F32), -1, keepdims=True)
        table = table_ref[...]
        picked = jnp.where(lane_ids(table.shape) == steps_ref[0], table, 0.0)
        coefs = jnp.broadcast_to(jnp.sum(picked, -1, keepdims=True), (2, LANES))
        c0 = jnp.broadcast_to(coefs[0:1], (8, LANES))
        c1 = jnp.broadcast_to(coefs[1:2], (8, LANES))
        coefs_ref[...] = jnp.concatenate([c0, c1], 0)
        pay = jnp.concatenate([lat_ref[...], c0], 0)
        for i in range(lat_pay_ref.shape[0]):
            lat_pay_ref[i] = pay

    at = pl.ds(pl.multiple_of(k * cols, cols), cols)
    w_in = w_in_ref[:, at]
    shift, scale, gate = mod_ref[0], mod_ref[1], mod_ref[2]
    inner = (w_in.astype(F32) - average[...]) * (1.0 + scale)
    shift_rows = jnp.where(row_ids((8, cols)) == 0, jnp.broadcast_to(shift, (8, cols)), 0.0)
    tokens_in = split_rows(jnp.concatenate([inner, shift_rows], 0), 0, LANES - HD - 8)
    w_qkv = w_qkv_ref[...].reshape(3 * local_heads * HD, cols)
    proj_sum[...] += lax.dot_general(w_qkv, tokens_in, NT, preferred_element_type=F32)
    w_proj = w_proj_ref[...]
    gated = split_rows(w_proj.astype(F32) * gate, HD, 0)
    out_sum[...] += lax.dot_general(w_out_ref[...], gated, NT, preferred_element_type=F32)
    io_sum[...] += lax.dot_general(w_in, w_proj, NT, preferred_element_type=F32)

    @pl.when(k == pl.num_programs(0) - 1)
    def _():
        w_io_ref[...] = io_sum[...]
        proj = proj_sum[:, :LANES] + proj_sum[:, LANES:]
        out = out_sum[:, :LANES] + out_sum[:, LANES:]
        lanes = lane_ids((HD, LANES))
        rows = row_ids((16, LANES))
        extra = jnp.zeros((16, LANES), F32)
        for h in range(local_heads):
            at_q = h * HD
            at_k = (local_heads + h) * HD
            at_v = (2 * local_heads + h) * HD
            q_t = jnp.transpose(proj[at_q : at_q + HD])
            v_t = jnp.transpose(proj[at_v : at_v + HD])
            score = exact_dot(q_t, proj[at_k : at_k + HD]) * (LOG2E * HD**-0.5)
            value = exact_dot(v_t, out[at_q : at_q + HD])
            params_ref[h * HD : (h + 1) * HD] = jnp.where(
                lanes < HD, score[:HD], value[:HD]
            ).astype(BF16)
            score_row = jnp.broadcast_to(score[HD : HD + 1], (16, LANES))
            const_row = jnp.broadcast_to(jnp.transpose(score)[HD : HD + 1], (16, LANES))
            value_row = jnp.broadcast_to(value[HD : HD + 1], (16, LANES))
            extra += jnp.where(rows == h, score_row, 0.0)
            extra += jnp.where(rows == 4 + h, const_row, 0.0)
            extra += jnp.where(rows == 8, value_row, 0.0)
        params_ref[local_heads * HD :] = extra.astype(BF16)


def tokens_kernel(pos_ref, behind_ref, start_ref, w_in_ref, params_ref, pay_ref, own_ref, cur_ref):
    current_t = jnp.where(pos_ref[0] == 0, start_ref[...], behind_ref[...])
    cur_ref[...] = current_t
    rounded = jnp.transpose(current_t).astype(BF16)
    hidden = jnp.dot(rounded, w_in_ref[...], preferred_element_type=F32)
    centred = hidden - jnp.mean(hidden, -1, keepdims=True)
    variance = jnp.mean(centred * centred, -1, keepdims=True)
    scaled = rounded.astype(F32) * lax.rsqrt(variance + 1e-05)
    half = scaled.shape[0] // 2
    own = jnp.concatenate([scaled[:half], scaled[half:]], 1).astype(BF16)
    own_ref[...] = own
    pay = jnp.concatenate([own, params_ref[...]], 0)
    for i in range(pay_ref.shape[0]):
        pay_ref[i] = pay


def unpacked(pairs):
    lanes = lane_ids(pairs.shape)
    one = jnp.where(lanes == HD, 1.0, 0.0)
    first = jnp.where(lanes < HD, pairs, one)
    second = jnp.where(lanes < HD, pltpu.roll(pairs, HD, 1), one)
    return first, second


def attend_kernel(
    all_ref, own_ref, cur_ref, w_io_ref, coefs_ref, pay_ref, keys, keys_t, queries, sums, *, chunk
):
    groups, held, _ = all_ref.shape
    half = own_ref.shape[0]
    tokens = 2 * half
    local_heads = (held - half - 16) // HD
    rows = local_heads * tokens
    pairs = groups * half

    first, second = unpacked(all_ref[:, :half, :].reshape(pairs, LANES).astype(F32))
    keys[:pairs] = first.astype(BF16)
    keys[pairs:] = second.astype(BF16)
    keys_t[:, :pairs] = jnp.transpose(first).astype(BF16)
    keys_t[:, pairs:] = jnp.transpose(second).astype(BF16)
    key_norm = jnp.maximum(
        jnp.max(jnp.sum(first * first, -1, keepdims=True)),
        jnp.max(jnp.sum(second * second, -1, keepdims=True)),
    )
    own = jnp.concatenate(unpacked(own_ref[...].astype(F32)), 0)
    own_x = own[:, :HD].astype(BF16)
    lanes = lane_ids((tokens, LANES))

    def make_queries(j, norm):
        extra = all_ref[j, half + local_heads * HD :].astype(F32)
        for h in range(local_heads):
            at = half + h * HD
            q = jnp.dot(own_x, all_ref[j, at : at + HD], preferred_element_type=F32)
            q += extra[h : h + 1]
            const = jnp.sum(own * extra[4 + h : 5 + h], -1, keepdims=True)
            q = jnp.where(lanes < HD, q, jnp.where(lanes == HD, const, 0.0)).astype(BF16)
            queries[j, h * tokens : (h + 1) * tokens] = q
            q = q.astype(F32)
            norm = jnp.maximum(norm, jnp.sum(q * q, -1, keepdims=True))
        return norm

    query_norm = jnp.max(lax.fori_loop(0, groups, make_queries, jnp.zeros((tokens, 1), F32)))
    safe = query_norm * key_norm <= SAFE * SAFE
    sums[...] = jnp.zeros_like(sums)

    def finish(j, weighted):
        mean = (weighted[:, :HD] / weighted[:, HD : HD + 1]).astype(BF16)
        total = sums[...]
        for h in range(local_heads):
            at = half + h * HD
            total += jnp.dot(
                mean[h * tokens : (h + 1) * tokens],
                all_ref[j, at : at + HD],
                preferred_element_type=F32,
            )
        total += all_ref[j, half + local_heads * HD + 8 : half + local_heads * HD + 16][
            0:1
        ].astype(F32)
        sums[...] = total

    @pl.when(safe)
    def _():
        def step(j, carry):
            q = queries[j]
            weighted = jnp.zeros((rows, LANES), F32)
            for c in range(0, 2 * pairs, chunk):
                s = jnp.dot(q, keys_t[:, c : c + chunk], preferred_element_type=F32)
                p = jnp.exp2(s).astype(BF16)
                weighted += jnp.dot(p, keys[c : c + chunk], preferred_element_type=F32)
            finish(j, weighted)
            return carry

        lax.fori_loop(0, groups, step, 0)

    @pl.when(jnp.logical_not(safe))
    def _():
        def step(j, carry):
            s = jnp.dot(queries[j], keys_t[...], preferred_element_type=F32)
            s = s - jnp.max(s, -1, keepdims=True)
            p = jnp.exp2(s).astype(BF16)
            finish(j, jnp.dot(p, keys[...], preferred_element_type=F32))
            return carry

        lax.fori_loop(0, groups, step, 0)

    attended_t = jnp.transpose(sums[...])[HD:]
    w_io_t = jnp.transpose(w_io_ref[...])
    embedded_t = exact_dot(w_io_t, cur_ref[...].astype(BF16).astype(F32))
    predicted = (coefs_ref[8:9] * (embedded_t + attended_t)).astype(BF16)
    for i in range(pay_ref.shape[0]):
        pay_ref[i] = predicted


def prefix_kernel(pos_ref, pred_ref, lat_ref, start_ref, out_ref, err_ref):
    window = pred_ref.shape[0]
    start = start_ref[...]
    refreshed = start
    own = start
    errors = jnp.zeros((1, LANES), F32)
    lanes = lane_ids((1, LANES))
    for s in range(window):
        current = start if s == 0 else lat_ref[s - 1, :HD]
        refreshed += lat_ref[s, HD : HD + 1] * current + pred_ref[s].astype(F32)
        difference = refreshed - lat_ref[s, :HD]
        error = jnp.sum(difference * difference, axis=(0, 1), keepdims=True)
        errors += jnp.where(lanes == s, error, 0.0)
        own = jnp.where(pos_ref[0] == s, refreshed, own)
    out_ref[...] = own
    for i in range(err_ref.shape[0]):
        err_ref[i] = errors


def vmem():
    return pl.BlockSpec(memory_space=pltpu.VMEM)


def smem():
    return pl.BlockSpec(memory_space=pltpu.SMEM)


def params_of(limit):
    return pltpu.CompilerParams(vmem_limit_bytes=limit * MIB)


def on_device(start, latents, time_mod, steps_window, ddim_table, w_in, w_qkv, w_attn_out, w_proj):
    own_rows = start.shape[0]
    window = lax.axis_size("tm")
    groups = lax.axis_size("head")
    d = w_in.shape[1]
    units = w_qkv.shape[1]
    local_heads = units // HD
    half = own_rows // 2
    held = units + 16
    pos = lax.axis_index("tm").astype(jnp.int32).reshape(1)
    start_t = start.T
    lat_t = latents[0].T
    behind_t = lax.ppermute(lat_t, "tm", [(i, i + 1) for i in range(window - 1)])

    cols = 1024
    whole = lambda *shape: pl.BlockSpec(shape, lambda k: (0,) * len(shape))
    params, w_io, lat_pay, coefs = pl.pallas_call(
        weights_kernel,
        grid=(d // cols,),
        in_specs=[
            smem(),
            pl.BlockSpec((3, 1, cols), lambda k: (0, 0, k)),
            whole(HD, d),
            pl.BlockSpec((3, units, cols), lambda k: (0, 0, k)),
            pl.BlockSpec((units, cols), lambda k: (0, k)),
            pl.BlockSpec((HD, cols), lambda k: (0, k)),
            whole(HD, own_rows),
            whole(2, ddim_table.shape[0]),
        ],
        out_specs=[
            whole(held, LANES),
            whole(HD, HD),
            whole(window, HD + 8, LANES),
            whole(16, LANES),
        ],
        out_shape=[
            jax.ShapeDtypeStruct((held, LANES), BF16),
            jax.ShapeDtypeStruct((HD, HD), F32),
            jax.ShapeDtypeStruct((window, HD + 8, LANES), F32),
            jax.ShapeDtypeStruct((16, LANES), F32),
        ],
        scratch_shapes=[
            pltpu.VMEM((3 * units, 2 * LANES), F32),
            pltpu.VMEM((units, 2 * LANES), F32),
            pltpu.VMEM((HD, HD), F32),
            pltpu.VMEM((HD, 1), F32),
        ],
        compiler_params=params_of(40),
        cost_estimate=pl.CostEstimate(
            flops=2 * d * 4 * units * 256, bytes_accessed=8 * units * d, transcendentals=0
        ),
        name="weights",
    )(
        steps_window,
        time_mod.transpose(1, 0, 2),
        w_in,
        w_qkv,
        w_attn_out,
        w_proj.T,
        lat_t,
        ddim_table.T,
    )

    pay, own, cur_t = pl.pallas_call(
        tokens_kernel,
        in_specs=[smem(), vmem(), vmem(), vmem(), vmem()],
        out_specs=[vmem(), vmem(), vmem()],
        out_shape=[
            jax.ShapeDtypeStruct((groups, half + held, LANES), BF16),
            jax.ShapeDtypeStruct((half, LANES), BF16),
            jax.ShapeDtypeStruct((HD, own_rows), F32),
        ],
        compiler_params=params_of(32),
        name="tokens",
    )(pos, behind_t, start_t, w_in, params)

    gathered = lax.all_to_all(pay, "head", 0, 0, tiled=True)
    lat_all = lax.all_to_all(lat_pay, "tm", 0, 0, tiled=True)

    seq = groups * own_rows
    pred_pay = pl.pallas_call(
        functools.partial(attend_kernel, chunk=256),
        in_specs=[vmem()] * 5,
        out_specs=vmem(),
        out_shape=jax.ShapeDtypeStruct((window, HD, own_rows), BF16),
        scratch_shapes=[
            pltpu.VMEM((seq, LANES), BF16),
            pltpu.VMEM((LANES, seq), BF16),
            pltpu.VMEM((groups, local_heads * own_rows, LANES), BF16),
            pltpu.VMEM((own_rows, LANES), F32),
        ],
        compiler_params=params_of(48),
        cost_estimate=pl.CostEstimate(
            flops=2 * groups * local_heads * own_rows * seq * 512,
            bytes_accessed=4 * MIB,
            transcendentals=groups * local_heads * own_rows * seq,
        ),
        name="attend",
    )(gathered, own, cur_t, w_io, coefs)

    pred_all = lax.all_to_all(pred_pay, "tm", 0, 0, tiled=True)
    refreshed_t, err_pay = pl.pallas_call(
        prefix_kernel,
        in_specs=[smem(), vmem(), vmem(), vmem()],
        out_specs=[vmem(), vmem()],
        out_shape=[
            jax.ShapeDtypeStruct((HD, own_rows), F32),
            jax.ShapeDtypeStruct((groups, 1, LANES), F32),
        ],
        compiler_params=params_of(32),
        name="prefix",
    )(pos, pred_all, lat_all, start_t)
    errors = lax.all_to_all(err_pay, "head", 0, 0, tiled=True)
    worst = jnp.max(jnp.sum(errors, axis=(0, 1)))
    return refreshed_t.T[None], worst / (seq * HD)


def solution(mesh):
    in_specs = (
        P("head", None),
        P("tm", "head", None),
        P("tm", None, None),
        P("tm"),
        P(),
        P(),
        P(None, "head", None),
        P("head", None),
        P(),
    )
    out_specs = (P("tm", "head", None), P())
    return jax.shard_map(
        on_device, mesh=mesh, in_specs=in_specs, out_specs=out_specs, check_vma=False
    )
```

time: 445 us -> 120 us (0.27)
  waiting for transfers between devices: 163 us -> 0.01 us
  matrix products: 101 us -> 0 us
  blocking collectives: 105 us -> 51.8 us
  Pallas kernels: 0 us -> 42 us
  other arithmetic: 31.6 us -> 0.64 us
  between operations: 16.7 us -> 3.11 us
  local copies, waits for them, and re-layouts: 18.4 us -> 7.48 us
  starting transfers between devices: 5.24 us -> 14.7 us
    reduce_scatter x1 -> x0, waiting for transfers between devices: 163 us -> none  [on_device(): lax.psum_scatter(jnp.dot(attended, w_attn_out, preferred_element_type=jnp...]
    dot_general x9 -> x0, matrix products: 63.8 us -> none  [the longest x4 29.9 us: attend_block(): jnp.einsum('hqk,khd->qhd', weights, per_head[2], preferred_element_type=j...]
    all_to_all x0 -> x3, blocking collectives: none -> 51.8 us  [the longest x1 23.7 us: on_device(): gathered = lax.all_to_all(pay, 'head', 0, 0, tiled=True)]
    pallas_call x0 -> x4, Pallas kernels: none -> 42 us  [the longest x1 36.2 us: on_device(): pl.pallas_call(functools.partial(attend_kernel, chunk=256), in_specs=[vme...]
    all_gather x2 -> x0, blocking collectives: 41.9 us -> none  [the longest x1 20.9 us: entering(): everything = lax.all_gather(x, axis)]
    sub x4 -> x0, matrix products: 37.2 us -> none  [attend_block(): weights = jax.nn.softmax(scores, -1).astype(jnp.bfloat16)]
    psum x1 -> x0, blocking collectives: 31.8 us -> none  [on_device(): summed = lax.psum(own_error, 'head')]
    pmax x1 -> x0, blocking collectives: 30.9 us -> none  [on_device(): largest = lax.pmax(summed, 'tm')]
  transfers between devices with their start and end apart: 2 -> 2, of which waited for: 1 -> 0; matrix products, arithmetic and copies ran while one was open for 1% -> 0% of each run, Pallas kernels for 0% -> 34%
where the time goes in v1:
time: 120 us
  blocking collectives  51.8 us (43%)
  Pallas kernels  42 us (35%)
  starting transfers between devices  14.7 us (12%)
  local copies, waits for them, and re-layouts  7.48 us (6%)
  between operations  3.11 us (3%)
    pallas_call x1, Pallas kernels, on_device(): pl.pallas_call(functools.partial(attend_kernel, chunk=256), in_specs=[vme...  36.2 us
    all_to_all x1, blocking collectives, on_device(): gathered = lax.all_to_all(pay, 'head', 0, 0, tiled=True)  23.7 us
    all_to_all x1, blocking collectives, on_device(): pred_all = lax.all_to_all(pred_pay, 'tm', 0, 0, tiled=True)  18.7 us
    all_to_all x1, starting transfers between devices, on_device(): lat_all = lax.all_to_all(lat_pay, 'tm', 0, 0, tiled=True)  9.77 us
    all_to_all x1, blocking collectives, on_device(): errors = lax.all_to_all(err_pay, 'head', 0, 0, tiled=True)  9.37 us
    unnamed x18, local copies, waits for them, and re-layouts  7.48 us
    ppermute x1, starting transfers between devices, on_device(): lax.ppermute(lat_t, 'tm', [(i, i + 1) for i in range(window - 1)])  4.94 us
    pallas_call x1, Pallas kernels, on_device(): pl.pallas_call(weights_kernel, grid=(d // cols,), in_specs=[smem(), pl.Bl...  4.22 us
  transfers between devices with their start and end apart: 2, of which 0 were waited for; matrix products, arithmetic and copies ran while one was open for 0% of the time, Pallas kernels for 34%

profile of v1, /device:TPU:1, one launch (start us, length us, event | category | flops | bytes accessed | tf_op | source)
XLA Modules:
  0.0 119.8 jit_solution(7354466937655962003)
XLA Ops:
  0.6 4.9 %collective-permute-start = (f32[64,128]{1,0:T(8,128)}, f32[64,128]{1,0:T(8,128)S(1)}, u32[]{:S(2)}, u32[]{:S(2)}) collective-permute-start(f32[64,128]{1,0:T(8,128)} %bitcast.15), channel_id=1, source_target_pairs={{0,16},{16,32},{32,48},{48,64},{64,80},{80,96},{96,112},{112,128},... | collective-permute-start | bytes 98312 | tf_op jit(solution)/shard_map/ppermute | solution.py:266
  6.2 0.0 copy-start
  6.2 2.0 %copy-done = bf16[3,192,3072]{2,1,0:T(8,128)(2,1)S(1)} copy-done((bf16[3,192,3072]{2,1,0:T(8,128)(2,1)S(1)}, bf16[3,192,3072]{2,1,0:T(8,128)(2,1)}, u32[]{:S(2)}) %copy-start) | copy-done | bytes 3538968
  8.2 0.0 copy-start.1
  8.2 1.0 copy-done.1
  9.2 0.0 copy-start.3
  9.2 1.3 %copy-done.3 = bf16[192,3072]{1,0:T(8,128)(2,1)S(1)} copy-done((bf16[192,3072]{1,0:T(8,128)(2,1)S(1)}, bf16[192,3072]{1,0:T(8,128)(2,1)}, u32[]{:S(2)}) %copy-start.3) | copy-done | bytes 1179672
  10.5 0.0 copy-start.4
  10.5 1.0 copy-done.4
  11.5 0.0 copy-start.6
  11.5 0.8 copy-done.6
  12.3 0.0 copy-start.7
  12.3 0.8 copy-done.7
  13.0 0.0 copy-start.8
  13.0 0.7 copy-done.8
  13.7 0.0 copy-start.2
  13.7 0.0 copy-start.5
  13.7 4.2 %weights.1 = (bf16[208,128]{1,0:T(8,128)(2,1)S(1)}, f32[64,64]{1,0:T(8,128)S(1)}, f32[16,72,128]{2,1,0:T(8,128)}, f32[16,128]{1,0:T(8,128)S(1)}) custom-call(s32[1]{0:T(128)S(6)} %copy.11.steps_ref, f32[3,1,3072]{2,1,0:T(1,128)S(1)} %bitcast.14, bf16[64,3072]{1,0:T(8,128)(2,1)S(1)} %copy-done.1, bf16[3,192,3072]{2,1,0:T(8,128)(2,1)S(1)} %copy-done, ...), custom_call_target="tpu_custom_call" | custom-call | flops 1207959552 | bytes 4718592 | tf_op jit(solution)/shard_map/weights/pallas_call | solution.py:270
  17.9 0.0 collective-permute-done.behind_ref
  17.9 0.0 copy-done.2
  17.9 0.0 copy-done.5
  17.9 0.8 tokens.1
  18.7 23.7 %all_to_all.20.all_ref = bf16[16,272,128]{2,1,0:T(8,128)(2,1)S(1)} all-to-all(bf16[16,272,128]{2,1,0:T(8,128)(2,1)S(1)} %get-tuple-element.12), channel_id=1, replica_groups=mesh['tm'=16,'head'=16] {'head'}, dimensions={0} | all-to-all | bytes 2228224 | tf_op jit(solution)/shard_map/all_to_all | solution.py:330
  42.5 9.8 %all-to-all-start.2 = ((f32[16,72,128]{2,1,0:T(8,128)}), f32[16,72,128]{2,1,0:T(8,128)S(1)}, u32[]{:S(2)}, u32[]{:S(2)}) async-start(f32[16,72,128]{2,1,0:T(8,128)} %get-tuple-element.17), calls=%async_computation.2 | async-start | bytes 1179648 | tf_op jit(solution)/shard_map/all_to_all | solution.py:331
  52.2 36.2 %attend.1 = bf16[16,64,128]{2,1,0:T(8,128)(2,1)S(1)} custom-call(bf16[16,272,128]{2,1,0:T(8,128)(2,1)S(1)} %all_to_all.20.all_ref, bf16[64,128]{1,0:T(8,128)(2,1)S(1)} %get-tuple-element.13.own_ref, f32[64,128]{1,0:T(8,128)S(1)} %get-tuple-element.14.cur_ref, f32[64,64]{1,0:T(8,128)S(1)} %get-tuple-element.15.w_io_ref, f32[16,128]{1,0:T(8,128)S(1)} %get-tuple-element.16.coefs_ref), custom_call_target="tpu_custom_call" | custom-call | flops 12884901888 | bytes 4194304 | tf_op jit(solution)/shard_map/attend/pallas_call | solution.py:334
  88.5 0.0 all-to-all-done.2.lat_ref
  88.5 18.7 %all_to_all.21.pred_ref = bf16[16,64,128]{2,1,0:T(8,128)(2,1)S(1)} all-to-all(bf16[16,64,128]{2,1,0:T(8,128)(2,1)S(1)} %attend.1), channel_id=1, replica_groups=mesh['tm'=16,'head'=16] {'tm'}, dimensions={0} | all-to-all | bytes 524288 | tf_op jit(solution)/shard_map/all_to_all | solution.py:354
  107.2 0.8 prefix.1
  108.0 9.4 %all_to_all.22 = f32[16,1,128]{2,1,0:T(1,128)S(1)} all-to-all(f32[16,1,128]{2,1,0:T(1,128)S(1)} %get-tuple-element.19), channel_id=1, replica_groups=mesh['tm'=16,'head'=16] {'head'}, dimensions={0} | all-to-all | bytes 16384 | tf_op jit(solution)/shard_map/all_to_all | solution.py:366
  117.4 0.6 reduce_max.9
  (1 shorter events, 0.0 us)
Async XLA Ops:
  0.6 17.3 %collective-permute-start = (f32[64,128]{1,0:T(8,128)}, f32[64,128]{1,0:T(8,128)S(1)}, u32[]{:S(2)}, u32[]{:S(2)}) collective-permute-start(f32[64,128]{1,0:T(8,128)} %bitcast.15), channel_id=1, source_target_pairs={{0,16},{16,32},{32,48},{48,64},{64,80},{80,96},{96,112},{112,128},... | collective-permute-start | bytes 98312 | tf_op jit(solution)/shard_map/ppermute | solution.py:266
  6.2 2.0 %copy-start = (bf16[3,192,3072]{2,1,0:T(8,128)(2,1)S(1)}, bf16[3,192,3072]{2,1,0:T(8,128)(2,1)}, u32[]{:S(2)}) copy-start(bf16[3,192,3072]{2,1,0:T(8,128)(2,1)} %w_qkv_ref.1) | copy-start | bytes 10616836
  8.2 1.0 copy-start.1
  9.2 1.3 %copy-start.3 = (bf16[192,3072]{1,0:T(8,128)(2,1)S(1)}, bf16[192,3072]{1,0:T(8,128)(2,1)}, u32[]{:S(2)}) copy-start(bf16[192,3072]{1,0:T(8,128)(2,1)} %w_out_ref.1) | copy-start | bytes 3538948
  10.5 1.0 copy-start.4
  11.5 0.8 copy-start.6
  12.3 0.8 copy-start.7
  13.0 0.7 copy-start.8
  13.7 4.2 %copy-start.2 = (bf16[64,3072]{1,0:T(8,128)(2,1)S(1)}, bf16[64,3072]{1,0:T(8,128)(2,1)}, u32[]{:S(2)}) copy-start(bf16[64,3072]{1,0:T(8,128)(2,1)} %w_in_ref.3) | copy-start | bytes 1179652
  13.7 4.2 %copy-start.5 = (f32[128,64]{0,1:T(8,128)S(1)}, f32[128,64]{0,1:T(8,128)}, u32[]{:S(2)}) copy-start(f32[128,64]{0,1:T(8,128)} %param.9) | copy-start | bytes 98308
  42.5 46.0 %all-to-all-start.2 = ((f32[16,72,128]{2,1,0:T(8,128)}), f32[16,72,128]{2,1,0:T(8,128)S(1)}, u32[]{:S(2)}, u32[]{:S(2)}) async-start(f32[16,72,128]{2,1,0:T(8,128)} %get-tuple-element.17), calls=%async_computation.2 | async-start | bytes 1179648 | tf_op jit(solution)/shard_map/all_to_all | solution.py:331

commit v2 on v1

v2 whole, which is shorter than its diff:
```python
import functools

import jax
import jax.numpy as jnp
from jax import lax
from jax.experimental import pallas as pl
from jax.experimental.pallas import tpu as pltpu
from jax.sharding import PartitionSpec as P

HD = 64
LANES = 128
LOG2E = 1.4426950408889634
SAFE = 100.0
F32 = jnp.float32
BF16 = jnp.bfloat16
NT = (((1,), (1,)), ((), ()))
MIB = 1 << 20


def lane_ids(shape):
    return lax.broadcasted_iota(jnp.int32, shape, len(shape) - 1)


def row_ids(shape):
    return lax.broadcasted_iota(jnp.int32, shape, 0)


def exact_dot(a, b):
    return jnp.dot(a, b, precision=lax.Precision.HIGHEST, preferred_element_type=F32)


def split_rows(values, before, after):
    head = values.astype(BF16)
    rest = (values - head.astype(F32)).astype(BF16)
    width = values.shape[1]
    parts = []
    for part in (head, rest):
        if before:
            parts.append(jnp.zeros((before, width), BF16))
        parts.append(part)
        if after:
            parts.append(jnp.zeros((after, width), BF16))
    return jnp.concatenate(parts, 0)


def weights_kernel(
    mod_ref, w_in_hbm, w_qkv_hbm, w_out_hbm, w_proj_hbm,
    params_ref, w_io_ref, w_in_ref, w_qkv_ref, w_out_ref, w_proj_ref, tokens_in, sems,
):
    local_heads = w_out_ref.shape[0] // HD
    cols = w_in_ref.shape[1]
    moves = [
        (w_in_hbm, w_in_ref),
        (w_qkv_hbm.at[0], w_qkv_ref.at[0]),
        (w_qkv_hbm.at[1], w_qkv_ref.at[1]),
        (w_proj_hbm, w_proj_ref),
        (w_out_hbm, w_out_ref),
        (w_qkv_hbm.at[2], w_qkv_ref.at[2]),
    ]
    copies = [pltpu.make_async_copy(a, b, sems.at[i]) for i, (a, b) in enumerate(moves)]
    for copy in copies:
        copy.start()

    shift, scale, gate = mod_ref[0], mod_ref[1], mod_ref[2]
    copies[0].wait()
    w_in = w_in_ref[...]
    wide = w_in.astype(F32)
    inner = (wide - jnp.mean(wide, -1, keepdims=True)) * (1.0 + scale)
    shift_rows = jnp.where(row_ids((8, cols)) == 0, jnp.broadcast_to(shift, (8, cols)), 0.0)
    tokens_in[...] = split_rows(
        jnp.concatenate([inner, shift_rows], 0), 0, LANES - HD - 8
    )

    def folded(w, by):
        both = lax.dot_general(w, by, NT, preferred_element_type=F32)
        return both[:, :LANES] + both[:, LANES:]

    copies[1].wait()
    proj_q = folded(w_qkv_ref[0], tokens_in[...])
    copies[2].wait()
    proj_k = folded(w_qkv_ref[1], tokens_in[...])
    copies[3].wait()
    w_proj = w_proj_ref[...]
    w_io_ref[...] = lax.dot_general(w_proj, w_in, NT, preferred_element_type=F32)
    gated = split_rows(w_proj.astype(F32) * gate, 0, HD)
    copies[4].wait()
    out = folded(w_out_ref[...], gated)
    copies[5].wait()
    proj_v = folded(w_qkv_ref[2], tokens_in[...])
    lanes = lane_ids((HD, LANES))
    rows = row_ids((16, LANES))
    extra = jnp.zeros((16, LANES), F32)
    maps = []
    for h in range(local_heads):
        at = h * HD
        k_t = jnp.transpose(proj_k[at : at + HD])
        o_t = jnp.transpose(out[at : at + HD])
        score = exact_dot(k_t, proj_q[at : at + HD]) * (LOG2E * HD**-0.5)
        value = exact_dot(o_t, proj_v[at : at + HD])
        maps.append(
            jnp.where(lanes < HD, score[:HD], pltpu.roll(value[:HD], HD, 1)).astype(BF16)
        )
        score_row = jnp.broadcast_to(jnp.transpose(score)[HD : HD + 1], (16, LANES))
        const_row = jnp.broadcast_to(score[HD : HD + 1], (16, LANES))
        value_row = jnp.broadcast_to(jnp.transpose(value)[HD : HD + 1], (16, LANES))
        extra += jnp.where(rows == h, score_row, 0.0)
        extra += jnp.where(rows == 4 + h, const_row, 0.0)
        extra += jnp.where(rows == 8, value_row, 0.0)
    params_ref[...] = jnp.concatenate(maps + [extra.astype(BF16)], 0)


def tokens_kernel(
    pos_ref, behind_ref, start_ref, w_in_ref, params_ref, pay_ref, own_ref, cur_ref, sems
):
    parts = pay_ref.shape[0]
    held = params_ref.shape[0]
    copies = []
    for i in range(parts):
        to = pay_ref.at[i, pl.ds(HD, held)]
        copies.append(pltpu.make_async_copy(params_ref, to, sems.at[0, i]))
        copies[-1].start()
    current_t = jnp.where(pos_ref[0] == 0, start_ref[...], behind_ref[...])
    cur_ref[...] = current_t
    rounded = jnp.transpose(current_t).astype(BF16)
    hidden = jnp.dot(rounded, w_in_ref[...], preferred_element_type=F32)
    centred = hidden - jnp.mean(hidden, -1, keepdims=True)
    variance = jnp.mean(centred * centred, -1, keepdims=True)
    scaled = rounded.astype(F32) * lax.rsqrt(variance + 1e-05)
    own_ref[...] = jnp.transpose(scaled).astype(BF16)
    for i in range(parts):
        to = pay_ref.at[i, pl.ds(0, HD)]
        copies.append(pltpu.make_async_copy(own_ref, to, sems.at[1, i]))
        copies[-1].start()
    for copy in copies:
        copy.wait()


def lat_kernel(steps_ref, lat_ref, table_ref, pay_ref, coefs_ref):
    table = table_ref[...]
    picked = jnp.where(lane_ids(table.shape) == steps_ref[0], table, 0.0)
    coefs = jnp.broadcast_to(jnp.sum(picked, -1, keepdims=True), (2, LANES))
    c0 = jnp.broadcast_to(coefs[0:1], (8, LANES))
    pay_ref[0] = jnp.concatenate([lat_ref[...], c0], 0)
    coefs_ref[...] = jnp.broadcast_to(coefs[1:2], (8, LANES))


def fill_keys(all_ref, keys, keys_v):
    groups = all_ref.shape[0]
    for j in range(groups):
        block = all_ref[j, :HD]
        width = block.shape[1]
        at = slice(j * width, (j + 1) * width)
        one = jnp.where(row_ids((HD, width)) == 0, 1.0, 0.0)
        keys[at] = jnp.transpose(jnp.concatenate([block.astype(F32), one], 0)).astype(BF16)
        keys_v[:, at] = jnp.concatenate([one.astype(BF16), block], 0)


def fill_queries(heads, maps_of, ex, own_t, queries):
    tokens = own_t.shape[1]
    one = jnp.where(row_ids((HD, tokens)) == 0, 1.0, 0.0).astype(BF16)
    x_only = jnp.concatenate([own_t, jnp.zeros_like(own_t)], 0)
    full = jnp.concatenate([own_t, one], 0)
    ex_t = jnp.transpose(ex.astype(F32))
    consts = jnp.dot(ex, full, preferred_element_type=F32)
    norm = jnp.zeros((1, tokens), F32)
    groups = ex.shape[0] // 16
    for h in range(heads):
        for j in range(groups):
            p = h * groups + j
            row = j * 16 + h
            part = jnp.dot(maps_of(h, j), x_only, preferred_element_type=F32)
            part = part + ex_t[:HD, row : row + 1]
            const = jnp.broadcast_to(consts[row + 4 : row + 5], (HD, tokens))
            const = jnp.where(row_ids((HD, tokens)) == 0, const, 0.0)
            column = jnp.concatenate([part, const], 0).astype(BF16)
            queries[:, p * tokens : (p + 1) * tokens] = column
            column = column.astype(F32)
            norm = jnp.maximum(norm, jnp.sum(column * column, 0, keepdims=True))
    return jnp.max(norm)


def attend(maps_of, groups, tokens, span, query_norm, keys, keys_v, queries, sums):
    aligned = keys_v[...].astype(F32)
    key_norm = jnp.max(jnp.sum(aligned * aligned, 0, keepdims=True))
    safe = query_norm * key_norm <= SAFE * SAFE
    pairs = span // tokens

    def run(terms):
        def step(i, carry):
            at = pl.ds(pl.multiple_of(i * span, span), span)
            s = jnp.dot(keys[...], queries[:, at], preferred_element_type=F32)
            weighted = jnp.dot(keys_v[...], terms(s), preferred_element_type=F32)
            mean = weighted * (1.0 / weighted[:1])
            mean = jnp.where(row_ids(mean.shape) >= HD, mean, 0.0).astype(BF16)
            h, j = lax.div(i * pairs, groups), lax.rem(i * pairs, groups)
            maps = [maps_of(h, j + p) for p in range(pairs)]
            means = [mean[:, p * tokens : (p + 1) * tokens] for p in range(pairs)]
            sums[...] += jnp.dot(
                jnp.concatenate(maps, 1),
                jnp.concatenate(means, 0),
                preferred_element_type=F32,
            )
            return carry

        lax.fori_loop(0, queries.shape[1] // span, step, 0)

    @pl.when(safe)
    def _():
        run(lambda s: jnp.exp2(s).astype(BF16))

    @pl.when(jnp.logical_not(safe))
    def _():
        run(lambda s: jnp.exp2(s - jnp.max(s, 0, keepdims=True)).astype(BF16))


def attend_kernel(
    all_ref, own_ref, cur_ref, w_io_ref, coefs_ref, pay_ref, keys, keys_v, queries, sums, *, span
):
    groups, held, _ = all_ref.shape
    heads = held // HD - 1
    fill_keys(all_ref, keys, keys_v)
    ex = all_ref[:, (1 + heads) * HD :, :].reshape(groups * 16, LANES)
    maps_of = lambda h, j: all_ref[j, (1 + h) * HD : (2 + h) * HD]
    norm = fill_queries(heads, maps_of, ex, own_ref[...], queries)
    ex_t = jnp.transpose(ex.astype(F32))[:HD]
    value = jnp.sum(jnp.where(lane_ids(ex_t.shape) % 16 == 8, ex_t, 0.0), -1, keepdims=True)
    embedded = exact_dot(w_io_ref[...], cur_ref[...].astype(BF16).astype(F32))
    sums[...] = embedded + value

    def maps_at(h, j):
        return all_ref[j, pl.ds(pl.multiple_of((1 + h) * HD, HD), HD)]

    attend(maps_at, groups, own_ref.shape[1], span, norm, keys, keys_v, queries, sums)
    predicted = (coefs_ref[:1] * sums[...]).astype(BF16)
    for i in range(pay_ref.shape[0]):
        pay_ref[i] = predicted


def mirrored(i):
    return (i & 1) * 8 + (i & 2) * 2 + ((i & 4) >> 1) + ((i & 8) >> 3)


def prefix_kernel(pos_ref, pred_ref, lat_ref, start_ref, out_ref, err_ref):
    window = pred_ref.shape[0]
    start = start_ref[...]
    refreshed = start
    current = start
    own = start
    errors = jnp.zeros((1, LANES), F32)
    lanes = lane_ids((1, LANES))
    for s in range(window):
        at = jnp.bitwise_xor(mirrored(pos_ref[0]), mirrored(s))
        refreshed += lat_ref[at, HD : HD + 1] * current + pred_ref[s].astype(F32)
        current = lat_ref[at, :HD]
        difference = refreshed - current
        error = jnp.sum(difference * difference, axis=(0, 1), keepdims=True)
        errors += jnp.where(lanes == s, error, 0.0)
        own = jnp.where(pos_ref[0] == s, refreshed, own)
    out_ref[...] = own
    for i in range(err_ref.shape[0]):
        err_ref[i] = errors


def vmem():
    return pl.BlockSpec(memory_space=pltpu.VMEM)


def smem():
    return pl.BlockSpec(memory_space=pltpu.SMEM)


def params_of(limit):
    return pltpu.CompilerParams(vmem_limit_bytes=limit * MIB)


def on_device(start, latents, time_mod, steps_window, ddim_table, w_in, w_qkv, w_attn_out, w_proj):
    own_rows = start.shape[0]
    window = lax.axis_size("tm")
    groups = lax.axis_size("head")
    d = w_in.shape[1]
    units = w_qkv.shape[1]
    local_heads = units // HD
    seq = groups * own_rows
    pos = lax.axis_index("tm").astype(jnp.int32).reshape(1)
    start_t = start.T
    lat_t = latents[0].T
    table_t = ddim_table.T
    behind_t = lax.ppermute(lat_t, "tm", [(i, i + 1) for i in range(window - 1)])

    lat_pay, coefs = pl.pallas_call(
        lat_kernel,
        in_specs=[smem(), vmem(), vmem()],
        out_specs=[vmem(), vmem()],
        out_shape=[
            jax.ShapeDtypeStruct((1, HD + 8, own_rows), F32),
            jax.ShapeDtypeStruct((8, LANES), F32),
        ],
        compiler_params=params_of(8),
        name="latents",
    )(steps_window, lat_t, table_t)

    held = units + 16
    in_hbm = lambda x: pltpu.with_memory_space_constraint(x, pltpu.HBM)
    hbm = pl.BlockSpec(memory_space=pltpu.HBM)
    params, w_io = pl.pallas_call(
        weights_kernel,
        in_specs=[vmem(), hbm, hbm, hbm, hbm],
        out_specs=[vmem(), vmem()],
        out_shape=[
            jax.ShapeDtypeStruct((held, LANES), BF16),
            jax.ShapeDtypeStruct((HD, HD), F32),
        ],
        scratch_shapes=[
            pltpu.VMEM((HD, d), BF16),
            pltpu.VMEM((3, units, d), BF16),
            pltpu.VMEM((units, d), BF16),
            pltpu.VMEM((HD, d), BF16),
            pltpu.VMEM((2 * LANES, d), BF16),
            pltpu.SemaphoreType.DMA((6,)),
        ],
        compiler_params=params_of(32),
        cost_estimate=pl.CostEstimate(
            flops=2 * d * 4 * units * 256, bytes_accessed=8 * units * d, transcendentals=0
        ),
        name="weights",
    )(
        time_mod.transpose(1, 0, 2),
        in_hbm(w_in),
        in_hbm(w_qkv),
        in_hbm(w_attn_out),
        in_hbm(w_proj.T),
    )

    pay, own, cur_t = pl.pallas_call(
        tokens_kernel,
        in_specs=[smem(), vmem(), vmem(), vmem(), vmem()],
        out_specs=[hbm, vmem(), vmem()],
        out_shape=[
            pltpu.HBM((groups, HD + held, LANES), BF16),
            jax.ShapeDtypeStruct((HD, own_rows), BF16),
            jax.ShapeDtypeStruct((HD, own_rows), F32),
        ],
        scratch_shapes=[pltpu.SemaphoreType.DMA((2, groups))],
        compiler_params=params_of(32),
        name="tokens",
    )(pos, behind_t, start_t, w_in, params)

    gathered = lax.all_to_all(pay, "head", 0, 0, tiled=True)
    lat_all = lat_pay
    for by in (8, 4, 2, 1):
        other = lax.ppermute(lat_all, "tm", [(i, i ^ by) for i in range(window)])
        lat_all = jnp.concatenate([lat_all, other], 0)

    span = 8 * own_rows

    pairs = groups * local_heads * own_rows * seq
    pred_pay = pl.pallas_call(
        functools.partial(attend_kernel, span=span),
        in_specs=[vmem()] * 5,
        out_specs=vmem(),
        out_shape=jax.ShapeDtypeStruct((window, HD, own_rows), BF16),
        scratch_shapes=[
            pltpu.VMEM((seq, LANES), BF16),
            pltpu.VMEM((LANES, seq), BF16),
            pltpu.VMEM((LANES, groups * local_heads * own_rows), BF16),
            pltpu.VMEM((HD, own_rows), F32),
        ],
        compiler_params=params_of(48),
        cost_estimate=pl.CostEstimate(
            flops=1024 * pairs, bytes_accessed=4 * MIB, transcendentals=pairs
        ),
        name="attend",
    )(gathered, own, cur_t, w_io, coefs)

    pred_all = lax.all_to_all(pred_pay, "tm", 0, 0, tiled=True)
    refreshed_t, err_pay = pl.pallas_call(
        prefix_kernel,
        in_specs=[smem(), vmem(), vmem(), vmem()],
        out_specs=[vmem(), vmem()],
        out_shape=[
            jax.ShapeDtypeStruct((HD, own_rows), F32),
            jax.ShapeDtypeStruct((groups, 1, LANES), F32),
        ],
        compiler_params=params_of(32),
        name="prefix",
    )(pos, pred_all, lat_all, start_t)
    errors = lax.all_to_all(err_pay, "head", 0, 0, tiled=True)
    worst = jnp.max(jnp.sum(errors, axis=(0, 1)))
    return refreshed_t.T[None], worst / (seq * HD)


def solution(mesh):
    in_specs = (
        P("head", None),
        P("tm", "head", None),
        P("tm", None, None),
        P("tm"),
        P(),
        P(),
        P(None, "head", None),
        P("head", None),
        P(),
    )
    out_specs = (P("tm", "head", None), P())
    return jax.shard_map(
        on_device, mesh=mesh, in_specs=in_specs, out_specs=out_specs, check_vma=False
    )
```

time: 120 us -> 93.8 us (0.78)
  blocking collectives: 51.8 us -> 9.03 us
  starting transfers between devices: 14.7 us -> 34.3 us
  waiting for transfers between devices: 0.01 us -> 17.1 us
  Pallas kernels: 42 us -> 28.2 us
  local copies, waits for them, and re-layouts: 7.48 us -> 0.83 us
    all_to_all x2 -> x0, blocking collectives: 42.5 us -> none  [the longest x1 23.7 us: on_device(): gathered = lax.all_to_all(pay, 'head', 0, 0, tiled=True)]
    pallas_call x2 -> x3, Pallas kernels: 40.4 us -> 25.7 us  [the longest x1 20 us: on_device(): pl.pallas_call(functools.partial(attend_kernel, span=span), in_specs=[vme...]
    all_to_all x1 -> x2, waiting for transfers between devices: 0.01 us -> 11.9 us  [the longest x1 9.98 us: on_device(): pred_all = lax.all_to_all(pred_pay, 'tm', 0, 0, tiled=True)]
    ppermute x0 -> x4, starting transfers between devices: none -> 11.5 us  [on_device(): other = lax.ppermute(lat_all, 'tm', [(i, i ^ by) for i in range(window)])]
    all_to_all x1 -> x2, starting transfers between devices: 9.77 us -> 17.8 us  [the longest x1 11 us: on_device(): pred_all = lax.all_to_all(pred_pay, 'tm', 0, 0, tiled=True)]
    unnamed x18 -> x14, local copies, waits for them, and re-layouts: 7.48 us -> 0.81 us
    ppermute x0 -> x4, waiting for transfers between devices: none -> 5.22 us  [on_device(): other = lax.ppermute(lat_all, 'tm', [(i, i ^ by) for i in range(window)])]
  transfers between devices with their start and end apart: 2 -> 7, of which waited for: 0 -> 5; matrix products, arithmetic and copies ran while one was open for 0% -> 0% of each run, Pallas kernels for 34% -> 27%
where the time goes in v2:
time: 93.8 us; the launch traced here: 93.4 us
  starting transfers between devices  34.3 us (37%)
  Pallas kernels  28.2 us (30%)
  waiting for transfers between devices  17.1 us (18%)
  blocking collectives  9.03 us (10%)
  between operations  3.19 us (3%)
    pallas_call x1, Pallas kernels, on_device(): pl.pallas_call(functools.partial(attend_kernel, span=span), in_specs=[vme...  20 us
    ppermute x4, starting transfers between devices, on_device(): other = lax.ppermute(lat_all, 'tm', [(i, i ^ by) for i in range(window)])  11.5 us
    all_to_all x1, starting transfers between devices, on_device(): pred_all = lax.all_to_all(pred_pay, 'tm', 0, 0, tiled=True)  11 us
    all_to_all x1, waiting for transfers between devices, on_device(): pred_all = lax.all_to_all(pred_pay, 'tm', 0, 0, tiled=True)  9.98 us
    all_to_all x1, blocking collectives, on_device(): errors = lax.all_to_all(err_pay, 'head', 0, 0, tiled=True)  9.03 us
    all_to_all x1, starting transfers between devices, on_device(): gathered = lax.all_to_all(pay, 'head', 0, 0, tiled=True)  6.77 us
    pallas_call x1, Pallas kernels, on_device(): pl.pallas_call(weights_kernel, in_specs=[vmem(), hbm, hbm, hbm, hbm], out...  5.53 us
    ppermute x4, waiting for transfers between devices, on_device(): other = lax.ppermute(lat_all, 'tm', [(i, i ^ by) for i in range(window)])  5.22 us
  transfers between devices with their start and end apart: 7, of which 5 were waited for; matrix products, arithmetic and copies ran while one was open for 0% of the time, Pallas kernels for 27%

profile of v2, /device:TPU:1, one launch (start us, length us, event | category | flops | bytes accessed | tf_op | source)
XLA Modules:
  0.0 93.4 jit_solution(6161395895450344633)
XLA Ops:
  0.6 4.9 %collective-permute-start = (f32[64,128]{1,0:T(8,128)}, f32[64,128]{1,0:T(8,128)S(1)}, u32[]{:S(2)}, u32[]{:S(2)}) collective-permute-start(f32[64,128]{1,0:T(8,128)} %bitcast.14), channel_id=1, source_target_pairs={{0,16},{16,32},{32,48},{48,64},{64,80},{80,96},{96,112},{112,128},... | collective-permute-start | bytes 98312 | tf_op jit(solution)/shard_map/ppermute | solution.py:288
  5.6 0.0 copy-start.2
  5.6 0.8 copy-done.2
  6.3 0.0 copy-start
  6.3 0.0 copy-start.1
  6.4 5.5 %weights.1 = (bf16[208,128]{1,0:T(8,128)(2,1)S(1)}, f32[64,64]{1,0:T(8,128)S(1)}) custom-call(f32[3,1,3072]{2,1,0:T(1,128)S(1)} %bitcast.13, bf16[64,3072]{1,0:T(8,128)(2,1)} %w_in_ref.1, bf16[3,192,3072]{2,1,0:T(8,128)(2,1)} %w_qkv_hbm.1, bf16[192,3072]{1,0:T(8,128)(2,1)} %w_out_hbm.1, bf16[64,3072]{1,0:T(8,128)(2,1)} %bitcast.17), custom_call_target="tpu_custom_call" | custom-call | flops 1207959552 | bytes 4718592 | tf_op jit(solution)/shard_map/weights/pallas_call | solution.py:305
  11.9 0.0 collective-permute-done.behind_ref
  11.9 0.0 copy-done
  11.9 0.0 copy-done.1
  11.9 1.8 %tokens.1 = (bf16[16,272,128]{2,1,0:T(8,128)(2,1)}, bf16[64,128]{1,0:T(8,128)(2,1)S(1)}, f32[64,128]{1,0:T(8,128)S(1)}) custom-call(s32[1]{0:T(128)} %bitcast.pos_ref, f32[64,128]{1,0:T(8,128)S(1)} %collective-permute-done.behind_ref, f32[64,128]{1,0:T(8,128)S(1)} %bitcast.11, bf16[64,3072]{1,0:T(8,128)(2,1)S(1)} %copy-done, ...), custom_call_target="tpu_custom_call" | custom-call | tf_op jit(solution)/shard_map/tokens/pallas_call | solution.py:334
  13.7 0.0 copy-start.3
  13.7 0.0 copy-start.4
  13.8 6.8 %all-to-all-start = ((bf16[16,272,128]{2,1,0:T(8,128)(2,1)}), bf16[16,272,128]{2,1,0:T(8,128)(2,1)S(1)}, u32[]{:S(2)}, u32[]{:S(2)}) async-start(bf16[16,272,128]{2,1,0:T(8,128)(2,1)} %get-tuple-element.12), calls=%async_computation | async-start | bytes 2228224 | tf_op jit(solution)/shard_map/all_to_all | solution.py:348
  21.2 0.0 copy-done.3
  21.2 0.0 copy-done.4
  21.2 0.1 latents.1
  21.3 6.0 %collective-permute-start.1 = (f32[1,72,128]{2,1,0:T(8,128)S(1)}, f32[1,72,128]{2,1,0:T(8,128)S(1)}, u32[]{:S(2)}, u32[]{:S(2)}) collective-permute-start(f32[1,72,128]{2,1,0:T(8,128)S(1)} %get-tuple-element.17), channel_id=1, source_target_pairs={{0,128},{16,144},{32,160},{48,176},{64,192},{80,208},{96,224},{112... | collective-permute-start | bytes 110600 | tf_op jit(solution)/shard_map/ppermute | solution.py:351
  27.3 1.7 %collective-permute-done.1 = f32[1,72,128]{2,1,0:T(8,128)S(1)} collective-permute-done((f32[1,72,128]{2,1,0:T(8,128)S(1)}, f32[1,72,128]{2,1,0:T(8,128)S(1)}, u32[]{:S(2)}, u32[]{:S(2)}) %collective-permute-start.1) | collective-permute-done | bytes 36896 | tf_op jit(solution)/shard_map/ppermute | solution.py:351
  29.1 2.5 %collective-permute-start.2 = (f32[2,72,128]{2,1,0:T(8,128)S(1)}, f32[2,72,128]{2,1,0:T(8,128)S(1)}, u32[]{:S(2)}, u32[]{:S(2)}) collective-permute-start(f32[2,72,128]{2,1,0:T(8,128)S(1)} %pad_maximum_fusion.2), channel_id=1, source_target_pairs={{0,64},{16,80},{32,96},{48,112},{64,0},{80,16},{96,32},{112,48},{1... | collective-permute-start | bytes 221192 | tf_op jit(solution)/shard_map/ppermute | solution.py:351
  31.5 2.0 %collective-permute-done.2 = f32[2,72,128]{2,1,0:T(8,128)S(1)} collective-permute-done((f32[2,72,128]{2,1,0:T(8,128)S(1)}, f32[2,72,128]{2,1,0:T(8,128)S(1)}, u32[]{:S(2)}, u32[]{:S(2)}) %collective-permute-start.2) | collective-permute-done | bytes 73760 | tf_op jit(solution)/shard_map/ppermute | solution.py:351
  33.6 2.9 %collective-permute-start.3 = (f32[4,72,128]{2,1,0:T(8,128)S(1)}, f32[4,72,128]{2,1,0:T(8,128)S(1)}, u32[]{:S(2)}, u32[]{:S(2)}) collective-permute-start(f32[4,72,128]{2,1,0:T(8,128)S(1)} %pad_maximum_fusion.1), channel_id=1, source_target_pairs={{0,32},{16,48},{32,0},{48,16},{64,96},{80,112},{96,64},{112,80},{1... | collective-permute-start | bytes 442376 | tf_op jit(solution)/shard_map/ppermute | solution.py:351
  36.4 1.9 %all-to-all-done.all_ref = bf16[16,272,128]{2,1,0:T(8,128)(2,1)S(1)} async-done(((bf16[16,272,128]{2,1,0:T(8,128)(2,1)}), bf16[16,272,128]{2,1,0:T(8,128)(2,1)S(1)}, u32[]{:S(2)}, u32[]{:S(2)}) %all-to-all-start) | async-done | bytes 1114144 | tf_op jit(solution)/shard_map/all_to_all | solution.py:348
  38.4 20.0 %attend.1 = bf16[16,64,128]{2,1,0:T(8,128)(2,1)} custom-call(bf16[16,272,128]{2,1,0:T(8,128)(2,1)S(1)} %all-to-all-done.all_ref, bf16[64,128]{1,0:T(8,128)(2,1)S(1)} %get-tuple-element.13.own_ref, f32[64,128]{1,0:T(8,128)S(1)} %get-tuple-element.14.cur_ref, f32[64,64]{1,0:T(8,128)S(1)} %get-tuple-element.15.w_io_ref, f32[8,128]{1,0:T(8,128)S(1)} %get-tuple-element.16.coefs_ref), custom_call_target="tpu_custom_call" | custom-call | flops 12884901888 | bytes 4194304 | tf_op jit(solution)/shard_map/attend/pallas_call | solution.py:357
  58.4 11.0 %all-to-all-start.1 = ((bf16[16,64,128]{2,1,0:T(8,128)(2,1)}), bf16[16,64,128]{2,1,0:T(8,128)(2,1)S(1)}, u32[]{:S(2)}, u32[]{:S(2)}) async-start(bf16[16,64,128]{2,1,0:T(8,128)(2,1)} %attend.1), calls=%async_computation.1 | async-start | bytes 524288 | tf_op jit(solution)/shard_map/all_to_all | solution.py:375
  69.5 0.0 collective-permute-done.3
  69.5 0.2 collective-permute-start.4
  69.7 1.4 %collective-permute-done.4 = f32[8,72,128]{2,1,0:T(8,128)S(1)} collective-permute-done((f32[8,72,128]{2,1,0:T(8,128)S(1)}, f32[8,72,128]{2,1,0:T(8,128)S(1)}, u32[]{:S(2)}, u32[]{:S(2)}) %collective-permute-start.4) | collective-permute-done | bytes 294944 | tf_op jit(solution)/shard_map/ppermute | solution.py:351
  71.2 10.0 %all-to-all-done.1.pred_ref = bf16[16,64,128]{2,1,0:T(8,128)(2,1)S(1)} async-done(((bf16[16,64,128]{2,1,0:T(8,128)(2,1)}), bf16[16,64,128]{2,1,0:T(8,128)(2,1)S(1)}, u32[]{:S(2)}, u32[]{:S(2)}) %all-to-all-start.1) | async-done | bytes 262176 | tf_op jit(solution)/shard_map/all_to_all | solution.py:375
  81.2 0.8 prefix.1
  81.9 9.0 %all_to_all.15 = f32[16,1,128]{2,1,0:T(1,128)S(1)} all-to-all(f32[16,1,128]{2,1,0:T(1,128)S(1)} %get-tuple-element.19), channel_id=1, replica_groups=mesh['tm'=16,'head'=16] {'head'}, dimensions={0} | all-to-all | bytes 16384 | tf_op jit(solution)/shard_map/all_to_all | solution.py:387
  91.0 0.6 reduce_max.9
  (9 shorter events, 0.1 us)
Async XLA Ops:
  0.6 11.3 %collective-permute-start = (f32[64,128]{1,0:T(8,128)}, f32[64,128]{1,0:T(8,128)S(1)}, u32[]{:S(2)}, u32[]{:S(2)}) collective-permute-start(f32[64,128]{1,0:T(8,128)} %bitcast.14), channel_id=1, source_target_pairs={{0,16},{16,32},{32,48},{48,64},{64,80},{80,96},{96,112},{112,128},... | collective-permute-start | bytes 98312 | tf_op jit(solution)/shard_map/ppermute | solution.py:288
  5.6 0.8 copy-start.2
  6.3 5.6 %copy-start = (bf16[64,3072]{1,0:T(8,128)(2,1)S(1)}, bf16[64,3072]{1,0:T(8,128)(2,1)}, u32[]{:S(2)}) copy-start(bf16[64,3072]{1,0:T(8,128)(2,1)} %w_in_ref.1) | copy-start | bytes 1179652
  6.3 5.6 %copy-start.1 = (f32[128,64]{0,1:T(8,128)S(1)}, f32[128,64]{0,1:T(8,128)}, u32[]{:S(2)}) copy-start(f32[128,64]{0,1:T(8,128)} %param.9) | copy-start | bytes 98308
  13.7 7.5 %copy-start.3 = (f32[1,128,64]{1,2,0:T(8,128)S(1)}, f32[1,128,64]{1,2,0:T(8,128)}, u32[]{:S(2)}) copy-start(f32[1,128,64]{1,2,0:T(8,128)} %param.10) | copy-start | bytes 98308
  13.7 7.5 %copy-start.4 = (f32[1000,2]{0,1:T(2,128)S(1)}, f32[1000,2]{0,1:T(2,128)}, u32[]{:S(2)}) copy-start(f32[1000,2]{0,1:T(2,128)} %param.13) | copy-start | bytes 24004
  13.8 24.6 %all-to-all-start = ((bf16[16,272,128]{2,1,0:T(8,128)(2,1)}), bf16[16,272,128]{2,1,0:T(8,128)(2,1)S(1)}, u32[]{:S(2)}, u32[]{:S(2)}) async-start(bf16[16,272,128]{2,1,0:T(8,128)(2,1)} %get-tuple-element.12), calls=%async_computation | async-start | bytes 2228224 | tf_op jit(solution)/shard_map/all_to_all | solution.py:348
  21.3 7.8 %collective-permute-start.1 = (f32[1,72,128]{2,1,0:T(8,128)S(1)}, f32[1,72,128]{2,1,0:T(8,128)S(1)}, u32[]{:S(2)}, u32[]{:S(2)}) collective-permute-start(f32[1,72,128]{2,1,0:T(8,128)S(1)} %get-tuple-element.17), channel_id=1, source_target_pairs={{0,128},{16,144},{32,160},{48,176},{64,192},{80,208},{96,224},{112... | collective-permute-start | bytes 110600 | tf_op jit(solution)/shard_map/ppermute | solution.py:351
  29.1 4.5 %collective-permute-start.2 = (f32[2,72,128]{2,1,0:T(8,128)S(1)}, f32[2,72,128]{2,1,0:T(8,128)S(1)}, u32[]{:S(2)}, u32[]{:S(2)}) collective-permute-start(f32[2,72,128]{2,1,0:T(8,128)S(1)} %pad_maximum_fusion.2), channel_id=1, source_target_pairs={{0,64},{16,80},{32,96},{48,112},{64,0},{80,16},{96,32},{112,48},{1... | collective-permute-start | bytes 221192 | tf_op jit(solution)/shard_map/ppermute | solution.py:351
  33.6 35.9 %collective-permute-start.3 = (f32[4,72,128]{2,1,0:T(8,128)S(1)}, f32[4,72,128]{2,1,0:T(8,128)S(1)}, u32[]{:S(2)}, u32[]{:S(2)}) collective-permute-start(f32[4,72,128]{2,1,0:T(8,128)S(1)} %pad_maximum_fusion.1), channel_id=1, source_target_pairs={{0,32},{16,48},{32,0},{48,16},{64,96},{80,112},{96,64},{112,80},{1... | collective-permute-start | bytes 442376 | tf_op jit(solution)/shard_map/ppermute | solution.py:351
  58.4 22.7 %all-to-all-start.1 = ((bf16[16,64,128]{2,1,0:T(8,128)(2,1)}), bf16[16,64,128]{2,1,0:T(8,128)(2,1)S(1)}, u32[]{:S(2)}, u32[]{:S(2)}) async-start(bf16[16,64,128]{2,1,0:T(8,128)(2,1)} %attend.1), calls=%async_computation.1 | async-start | bytes 524288 | tf_op jit(solution)/shard_map/all_to_all | solution.py:375
  69.5 1.7 %collective-permute-start.4 = (f32[8,72,128]{2,1,0:T(8,128)S(1)}, f32[8,72,128]{2,1,0:T(8,128)S(1)}, u32[]{:S(2)}, u32[]{:S(2)}) collective-permute-start(f32[8,72,128]{2,1,0:T(8,128)S(1)} %pad_maximum_fusion), channel_id=1, source_target_pairs={{0,16},{16,0},{32,48},{48,32},{64,80},{80,64},{96,112},{112,96},{1... | collective-permute-start | bytes 884744 | tf_op jit(solution)/shard_map/ppermute | solution.py:351

commit v3 on v2

v3 whole, which is shorter than its diff:
```python
import functools

import jax
import jax.numpy as jnp
from jax import lax
from jax.experimental import pallas as pl
from jax.experimental.pallas import tpu as pltpu
from jax.sharding import PartitionSpec as P

HD = 64
LANES = 128
LOG2E = 1.4426950408889634
SAFE = 100.0
F32 = jnp.float32
BF16 = jnp.bfloat16
NT = (((1,), (1,)), ((), ()))
MIB = 1 << 20


def lane_ids(shape):
    return lax.broadcasted_iota(jnp.int32, shape, len(shape) - 1)


def row_ids(shape):
    return lax.broadcasted_iota(jnp.int32, shape, 0)


def close_dot(a, b):
    a_head, b_head = a.astype(BF16), b.astype(BF16)
    a_rest = (a - a_head.astype(F32)).astype(BF16)
    b_rest = (b - b_head.astype(F32)).astype(BF16)
    dot = functools.partial(jnp.dot, preferred_element_type=F32)
    return dot(a_head, b_head) + (dot(a_head, b_rest) + dot(a_rest, b_head))


def split_rows(values, before, after):
    head = values.astype(BF16)
    rest = (values - head.astype(F32)).astype(BF16)
    width = values.shape[1]
    parts = []
    for part in (head, rest):
        if before:
            parts.append(jnp.zeros((before, width), BF16))
        parts.append(part)
        if after:
            parts.append(jnp.zeros((after, width), BF16))
    return jnp.concatenate(parts, 0)


def weights_kernel(
    mod_ref, w_in_ref, w_qkv_hbm, w_out_hbm, w_proj_hbm,
    score_ref, value_ref, w_io_ref, w_qkv_ref, w_out_ref, w_proj_ref, tokens_in, sems,
):
    local_heads = w_out_ref.shape[0] // HD
    cols = w_in_ref.shape[1]
    moves = [
        (w_proj_hbm, w_proj_ref),
        (w_out_hbm, w_out_ref),
        (w_qkv_hbm.at[0], w_qkv_ref.at[0]),
        (w_qkv_hbm.at[1], w_qkv_ref.at[1]),
        (w_qkv_hbm.at[2], w_qkv_ref.at[2]),
    ]
    copies = [pltpu.make_async_copy(a, b, sems.at[i]) for i, (a, b) in enumerate(moves)]
    for copy in copies:
        copy.start()

    shift, scale, gate = mod_ref[0], mod_ref[1], mod_ref[2]
    w_in = w_in_ref[...]
    wide = w_in.astype(F32)
    inner = (wide - jnp.mean(wide, -1, keepdims=True)) * (1.0 + scale)
    shift_rows = jnp.where(row_ids((8, cols)) == 0, jnp.broadcast_to(shift, (8, cols)), 0.0)
    tokens_in[...] = split_rows(
        jnp.concatenate([inner, shift_rows], 0), 0, LANES - HD - 8
    )

    def folded(w, by):
        both = lax.dot_general(w, by, NT, preferred_element_type=F32)
        return both[:, :LANES] + both[:, LANES:]

    copies[0].wait()
    w_proj = w_proj_ref[...]
    w_io_ref[...] = lax.dot_general(w_proj, w_in, NT, preferred_element_type=F32)
    gated = split_rows(w_proj.astype(F32) * gate, 0, HD)
    copies[1].wait()
    out = folded(w_out_ref[...], gated)
    units = w_qkv_ref.shape[1]
    for copy in copies[2:]:
        copy.wait()
    proj = folded(w_qkv_ref[...].reshape(3 * units, cols), tokens_in[...])
    proj_q, proj_k, proj_v = proj[:units], proj[units : 2 * units], proj[2 * units :]
    for h in range(local_heads):
        at = slice(h * HD, (h + 1) * HD)
        score = close_dot(jnp.transpose(proj_k[at]), proj_q[at]) * (LOG2E * HD**-0.5)
        value = close_dot(jnp.transpose(out[at])[:HD], proj_v[at])
        score_ref[h] = score.astype(BF16)
        value_ref[h] = value.astype(BF16)


def tokens_kernel(
    last_ref, steps_hbm, lat_hbm, table_hbm, w_in_hbm, start_hbm,
    pay_ref, cur_ref, lat_ref, w_in_ref, start_ref, own_ref, table_ref, steps_ref, sems,
):
    moves = [
        (lat_hbm, lat_ref.at[0, pl.ds(0, HD)]),
        (start_hbm, start_ref),
        (w_in_hbm, w_in_ref),
        (steps_hbm, steps_ref),
        (table_hbm, table_ref),
    ]
    parts = pay_ref.shape[0]
    copies = [pltpu.make_async_copy(a, b, sems.at[parts + i]) for i, (a, b) in enumerate(moves)]
    for copy in copies:
        copy.start()
    for copy in copies[:3]:
        copy.wait()
    current_t = jnp.where(last_ref[0] == 1, start_ref[...], lat_ref[0, :HD])
    cur_ref[...] = current_t
    rounded = jnp.transpose(current_t).astype(BF16)
    hidden = jnp.dot(rounded, w_in_ref[...], preferred_element_type=F32)
    centred = hidden - jnp.mean(hidden, -1, keepdims=True)
    variance = jnp.mean(centred * centred, -1, keepdims=True)
    scaled = rounded.astype(F32) * lax.rsqrt(variance + 1e-05)
    own_ref[...] = jnp.transpose(scaled).astype(BF16)
    sends = [pltpu.make_async_copy(own_ref, pay_ref.at[i], sems.at[i]) for i in range(parts)]
    for send in sends:
        send.start()
    for copy in copies[3:]:
        copy.wait()
    table = table_ref[...]
    picked = jnp.where(lane_ids(table.shape) == steps_ref[0], table, 0.0)
    coefs = jnp.broadcast_to(jnp.sum(picked, -1, keepdims=True), (2, LANES))
    lat_ref[0, pl.ds(HD, 8)] = jnp.concatenate([coefs] * 4, 0)
    for send in sends:
        send.wait()


def attend_kernel(all_ref, score_ref, value_ref, pay_ref, keys, keys_t, queries, sums, *, span):
    groups, _, tokens = all_ref.shape
    heads = score_ref.shape[0]
    seq = keys.shape[0]
    for j in range(groups):
        at = slice(j * tokens, (j + 1) * tokens)
        block = all_ref[j].astype(F32)
        one = jnp.where(row_ids(block.shape) == 0, 1.0, 0.0)
        block = jnp.concatenate([block, one], 0).astype(BF16)
        keys[at] = jnp.transpose(block)
        keys_t[:, at] = block

    def longest(columns):
        columns = columns.astype(F32)
        return jnp.max(jnp.sum(columns * columns, 0, keepdims=True))

    query_norm = 0.0
    for h in range(heads):
        columns = jnp.dot(score_ref[h], keys_t[...], preferred_element_type=F32).astype(BF16)
        queries[h] = columns
        query_norm = jnp.maximum(query_norm, longest(columns))
    safe = query_norm * longest(keys_t[...]) <= SAFE * SAFE
    sums[...] = jnp.zeros_like(sums)

    def run(terms):
        def step(i, carry):
            h = lax.rem(i, heads)
            at = pl.ds(pl.multiple_of(lax.div(i, heads) * span, span), span)
            s = jnp.dot(keys[...], queries[h, :, at], preferred_element_type=F32)
            weighted = jnp.dot(keys_t[...], terms(s), preferred_element_type=F32)
            mean = (weighted * (1.0 / weighted[HD : HD + 1])).astype(BF16)
            sums[:, at] += jnp.dot(value_ref[h], mean, preferred_element_type=F32)
            return carry

        lax.fori_loop(0, heads * (seq // span), step, 0)

    @pl.when(safe)
    def _():
        run(lambda s: jnp.exp2(s).astype(BF16))

    @pl.when(jnp.logical_not(safe))
    def _():
        run(lambda s: jnp.exp2(s - jnp.max(s, 0, keepdims=True)).astype(BF16))

    for j in range(groups):
        pay_ref[j] = sums[:, j * tokens : (j + 1) * tokens].astype(BF16)


def predict_kernel(shares_ref, cur_ref, w_io_ref, pay_ref):
    total = close_dot(w_io_ref[...], cur_ref[...].astype(BF16).astype(F32))
    for j in range(shares_ref.shape[0]):
        total += shares_ref[j].astype(F32)
    predicted = total.astype(BF16)
    for i in range(pay_ref.shape[0]):
        pay_ref[i] = predicted


def mirrored(i):
    return (i & 1) * 8 + (i & 4) + ((i & 8) >> 2) + ((i & 2) >> 1)


def prefix_kernel(pos_ref, pred_ref, lat_ref, start_ref, out_ref, err_ref):
    window = pred_ref.shape[0]
    start = start_ref[...]
    refreshed = start
    current = start
    own = start
    errors = jnp.zeros((1, LANES), F32)
    lanes = lane_ids((1, LANES))
    for s in range(window):
        at = jnp.bitwise_xor(mirrored(pos_ref[0]), mirrored(s))
        predicted = pred_ref[(s - 1) % window].astype(F32)
        c0, c1 = lat_ref[at, HD : HD + 1], lat_ref[at, HD + 1 : HD + 2]
        refreshed += c0 * current + c1 * predicted
        current = lat_ref[at, :HD]
        difference = refreshed - current
        error = jnp.sum(difference * difference, axis=(0, 1), keepdims=True)
        errors += jnp.where(lanes == s, error, 0.0)
        own = jnp.where(pos_ref[0] == s, refreshed, own)
    out_ref[...] = own
    for i in range(err_ref.shape[0]):
        err_ref[i] = errors


def vmem():
    return pl.BlockSpec(memory_space=pltpu.VMEM)


def smem():
    return pl.BlockSpec(memory_space=pltpu.SMEM)


def params_of(limit):
    return pltpu.CompilerParams(vmem_limit_bytes=limit * MIB)


def on_device(start, latents, time_mod, steps_window, ddim_table, w_in, w_qkv, w_attn_out, w_proj):
    own_rows = start.shape[0]
    window = lax.axis_size("tm")
    groups = lax.axis_size("head")
    d = w_in.shape[1]
    units = w_qkv.shape[1]
    local_heads = units // HD
    seq = groups * own_rows
    pos = lax.axis_index("tm").astype(jnp.int32).reshape(1)
    start_t = start.T
    lat_t = latents[0].T
    table_t = ddim_table.T
    mod = time_mod.transpose(1, 0, 2)

    in_hbm = lambda x: pltpu.with_memory_space_constraint(x, pltpu.HBM)
    hbm = pl.BlockSpec(memory_space=pltpu.HBM)
    last = (pos == window - 1).astype(jnp.int32)
    pay, cur_t, lat_pay, w_in_near, start_near = pl.pallas_call(
        tokens_kernel,
        in_specs=[smem(), pl.BlockSpec(memory_space=pl.ANY), hbm, hbm, hbm, hbm],
        out_specs=[hbm] + [vmem()] * 4,
        out_shape=[
            pltpu.HBM((groups, HD, own_rows), BF16),
            pltpu.VMEM((HD, own_rows), F32),
            pltpu.VMEM((1, HD + 8, own_rows), F32),
            pltpu.VMEM((HD, d), BF16),
            pltpu.VMEM((HD, own_rows), F32),
        ],
        scratch_shapes=[
            pltpu.VMEM((HD, own_rows), BF16),
            pltpu.VMEM((2, ddim_table.shape[0]), F32),
            pltpu.SMEM((1,), jnp.int32),
            pltpu.SemaphoreType.DMA((groups + 5,)),
        ],
        compiler_params=params_of(8),
        name="tokens",
    )(last, steps_window, in_hbm(lat_t), in_hbm(table_t), in_hbm(w_in), in_hbm(start_t))
    mod = lax.ppermute(mod, "tm", [(i, (i - 1) % window) for i in range(window)])
    tokens = lax.all_to_all(pay, "head", 0, 0, tiled=True)

    score, value, w_io = pl.pallas_call(
        weights_kernel,
        in_specs=[vmem(), vmem(), hbm, hbm, hbm],
        out_specs=[vmem()] * 3,
        out_shape=[
            jax.ShapeDtypeStruct((local_heads, LANES, LANES), BF16),
            jax.ShapeDtypeStruct((local_heads, HD, LANES), BF16),
            jax.ShapeDtypeStruct((HD, HD), F32),
        ],
        scratch_shapes=[
            pltpu.VMEM((3, units, d), BF16),
            pltpu.VMEM((units, d), BF16),
            pltpu.VMEM((HD, d), BF16),
            pltpu.VMEM((2 * LANES, d), BF16),
            pltpu.SemaphoreType.DMA((5,)),
        ],
        compiler_params=params_of(32),
        cost_estimate=pl.CostEstimate(
            flops=2 * d * 4 * units * 256, bytes_accessed=8 * units * d, transcendentals=0
        ),
        name="weights",
    )(
        mod,
        w_in_near,
        in_hbm(w_qkv),
        in_hbm(w_attn_out),
        in_hbm(w_proj.T),
    )

    pairs = local_heads * seq * seq
    def spread(entries, by):
        other = lax.ppermute(entries, "tm", [(i, i ^ by) for i in range(window)])
        return jnp.concatenate([entries, other], 0)

    lat_all = spread(lat_pay, 2)
    shares = pl.pallas_call(
        functools.partial(attend_kernel, span=seq),
        in_specs=[vmem()] * 3,
        out_specs=vmem(),
        out_shape=jax.ShapeDtypeStruct((groups, HD, own_rows), BF16),
        scratch_shapes=[
            pltpu.VMEM((seq, LANES), BF16),
            pltpu.VMEM((LANES, seq), BF16),
            pltpu.VMEM((local_heads, LANES, seq), BF16),
            pltpu.VMEM((HD, seq), F32),
        ],
        compiler_params=params_of(48),
        cost_estimate=pl.CostEstimate(
            flops=1024 * pairs, bytes_accessed=4 * MIB, transcendentals=pairs
        ),
        name="attend",
    )(tokens, score, value)

    shares, lat_all = lax.optimization_barrier((shares, lat_all))
    lat_all = spread(spread(spread(lat_all, 8), 4), 1)
    shares = lax.all_to_all(shares, "head", 0, 0, tiled=True)

    pred_pay = pl.pallas_call(
        predict_kernel,
        in_specs=[vmem()] * 3,
        out_specs=vmem(),
        out_shape=jax.ShapeDtypeStruct((window, HD, own_rows), BF16),
        compiler_params=params_of(32),
        name="predict",
    )(shares, cur_t, w_io)

    pred_all = lax.all_to_all(pred_pay, "tm", 0, 0, tiled=True)
    refreshed_t, err_pay = pl.pallas_call(
        prefix_kernel,
        in_specs=[smem(), vmem(), vmem(), vmem()],
        out_specs=[vmem(), vmem()],
        out_shape=[
            jax.ShapeDtypeStruct((HD, own_rows), F32),
            jax.ShapeDtypeStruct((groups, 1, LANES), F32),
        ],
        compiler_params=params_of(32),
        name="prefix",
    )(pos, pred_all, lat_all, start_near)
    errors = lax.all_to_all(err_pay, "head", 0, 0, tiled=True)
    worst = jnp.max(jnp.sum(errors, axis=(0, 1)))
    return refreshed_t.T[None], worst / (seq * HD)


def solution(mesh):
    in_specs = (
        P("head", None),
        P("tm", "head", None),
        P("tm", None, None),
        P("tm"),
        P(),
        P(),
        P(None, "head", None),
        P("head", None),
        P(),
    )
    out_specs = (P("tm", "head", None), P())
    return jax.shard_map(
        on_device, mesh=mesh, in_specs=in_specs, out_specs=out_specs, check_vma=False
    )
```

time: 93.8 us -> 89.2 us (0.951)
  starting transfers between devices: 34.3 us -> 29.8 us
  waiting for transfers between devices: 17.1 us -> 19.5 us
  Pallas kernels: 28.2 us -> 26.5 us
    all_to_all x1 -> x2, waiting for transfers between devices: 1.94 us -> 8.04 us  [the longest x1 6.54 us: on_device(): shares = lax.all_to_all(shares, 'head', 0, 0, tiled=True)]
    all_to_all x1, starting transfers between devices: 11 us -> 7.2 us  [on_device(): pred_all = lax.all_to_all(pred_pay, 'tm', 0, 0, tiled=True)]
    ppermute x5, waiting for transfers between devices: 5.22 us -> 1.49 us  [the longest x4 1.49 us: spread(): other = lax.ppermute(entries, 'tm', [(i, i ^ by) for i in range(window)])]
    ppermute x5, starting transfers between devices: 16.5 us -> 14 us  [the longest x4 10.8 us: spread(): other = lax.ppermute(entries, 'tm', [(i, i ^ by) for i in range(window)])]
    all_to_all x1 -> x2, starting transfers between devices: 6.77 us -> 8.56 us  [the longest x1 5.03 us: on_device(): tokens = lax.all_to_all(pay, 'head', 0, 0, tiled=True)]
    pallas_call x4, Pallas kernels: 27.5 us -> 25.7 us  [the longest x1 17.9 us: on_device(): pl.pallas_call(functools.partial(attend_kernel, span=seq), in_specs=[vmem...]
  transfers between devices with their start and end apart: 7 -> 8, of which waited for: 5 -> 4; matrix products, arithmetic and copies ran while one was open for 0% -> 0% of each run, Pallas kernels for 27% -> 9%
where the time goes in v3:
time: 89.2 us; the launch traced here: 88.6 us
  starting transfers between devices  29.8 us (33%)
  Pallas kernels  26.5 us (30%)
  waiting for transfers between devices  19.5 us (22%)
  blocking collectives  9.02 us (10%)
  between operations  3.14 us (4%)
    pallas_call x1, Pallas kernels, on_device(): pl.pallas_call(functools.partial(attend_kernel, span=seq), in_specs=[vmem...  17.9 us
    ppermute x4, starting transfers between devices, spread(): other = lax.ppermute(entries, 'tm', [(i, i ^ by) for i in range(window)])  10.8 us
    all_to_all x1, waiting for transfers between devices, on_device(): pred_all = lax.all_to_all(pred_pay, 'tm', 0, 0, tiled=True)  9.96 us
    all_to_all x1, blocking collectives, on_device(): errors = lax.all_to_all(err_pay, 'head', 0, 0, tiled=True)  9.02 us
    all_to_all x1, starting transfers between devices, on_device(): pred_all = lax.all_to_all(pred_pay, 'tm', 0, 0, tiled=True)  7.2 us
    all_to_all x1, waiting for transfers between devices, on_device(): shares = lax.all_to_all(shares, 'head', 0, 0, tiled=True)  6.54 us
    all_to_all x1, starting transfers between devices, on_device(): tokens = lax.all_to_all(pay, 'head', 0, 0, tiled=True)  5.03 us
    pallas_call x1, Pallas kernels, on_device(): pl.pallas_call(weights_kernel, in_specs=[vmem(), vmem(), hbm, hbm, hbm],...  4.28 us
  transfers between devices with their start and end apart: 8, of which 4 were waited for; matrix products, arithmetic and copies ran while one was open for 0% of the time, Pallas kernels for 9%

profile of v3, /device:TPU:1, one launch (start us, length us, event | category | flops | bytes accessed | tf_op | source)
XLA Modules:
  0.0 88.6 jit_solution(2764329036909278391)
XLA Ops:
  0.6 3.3 %collective-permute-start = (f32[3,1,3072]{2,1,0:T(1,128)}, f32[3,1,3072]{2,1,0:T(1,128)S(1)}, u32[]{:S(2)}, u32[]{:S(2)}) collective-permute-start(f32[3,1,3072]{2,1,0:T(1,128)} %bitcast.15), channel_id=1, source_target_pairs={{0,240},{16,0},{32,16},{48,32},{64,48},{80,64},{96,80},{112,96},{1... | collective-permute-start | bytes 110600 | tf_op jit(solution)/shard_map/ppermute | solution.py:270
  4.5 2.7 %tokens.1 = (bf16[16,64,128]{2,1,0:T(8,128)(2,1)}, f32[64,128]{1,0:T(8,128)S(1)}, f32[1,72,128]{2,1,0:T(8,128)S(1)}, bf16[64,3072]{1,0:T(8,128)(2,1)S(1)}, f32[64,128]{1,0:T(8,128)S(1)}) custom-call(s32[1]{0:T(128)S(6)} %convert_element_type.3.last_ref, s32[1]{0:T(128)S(6)} %copy.11.steps_hbm, f32[64,128]{1,0:T(8,128)} %bitcast.12, f32[2,1000]{1,0:T(2,128)} %bitcast.14, ...), custom_call_target="tpu_custom_call" | custom-call | tf_op jit(solution)/shard_map/tokens/pallas_call | solution.py:250
  7.2 5.0 %all-to-all-start = ((bf16[16,64,128]{2,1,0:T(8,128)(2,1)}), bf16[16,64,128]{2,1,0:T(8,128)(2,1)S(1)}, u32[]{:S(2)}, u32[]{:S(2)}) async-start(bf16[16,64,128]{2,1,0:T(8,128)(2,1)} %get-tuple-element.14), calls=%async_computation | async-start | bytes 524288 | tf_op jit(solution)/shard_map/all_to_all | solution.py:271
  12.3 1.7 %collective-permute-start.1 = (f32[1,72,128]{2,1,0:T(8,128)S(1)}, f32[1,72,128]{2,1,0:T(8,128)S(1)}, u32[]{:S(2)}, u32[]{:S(2)}) collective-permute-start(f32[1,72,128]{2,1,0:T(8,128)S(1)} %get-tuple-element.18), channel_id=1, source_target_pairs={{0,32},{16,48},{32,0},{48,16},{64,96},{80,112},{96,64},{112,80},{1... | collective-permute-start | bytes 110600 | tf_op jit(solution)/shard_map/ppermute | solution.py:304
  14.0 0.0 collective-permute-done.mod_ref
  14.0 4.3 %weights.1 = (bf16[3,128,128]{2,1,0:T(8,128)(2,1)S(1)}, bf16[3,64,128]{2,1,0:T(8,128)(2,1)S(1)}, f32[64,64]{1,0:T(8,128)S(1)}) custom-call(f32[3,1,3072]{2,1,0:T(1,128)S(1)} %collective-permute-done.mod_ref, bf16[64,3072]{1,0:T(8,128)(2,1)S(1)} %get-tuple-element.15.w_in_ref, bf16[3,192,3072]{2,1,0:T(8,128)(2,1)} %w_qkv_hbm.1, bf16[192,3072]{1,0:T(8,128)(2,1)} %w_out_hbm.1, ...), custom_call_target="tpu_custom_call" | custom-call | flops 1207959552 | bytes 4718592 | tf_op jit(solution)/shard_map/weights/pallas_call | solution.py:273
  18.3 0.0 collective-permute-done.1
  18.3 1.5 %all-to-all-done.all_ref = bf16[16,64,128]{2,1,0:T(8,128)(2,1)S(1)} async-done(((bf16[16,64,128]{2,1,0:T(8,128)(2,1)}), bf16[16,64,128]{2,1,0:T(8,128)(2,1)S(1)}, u32[]{:S(2)}, u32[]{:S(2)}) %all-to-all-start) | async-done | bytes 262176 | tf_op jit(solution)/shard_map/all_to_all | solution.py:271
  19.8 17.9 %attend.1 = bf16[16,64,128]{2,1,0:T(8,128)(2,1)} custom-call(bf16[16,64,128]{2,1,0:T(8,128)(2,1)S(1)} %all-to-all-done.all_ref, bf16[3,128,128]{2,1,0:T(8,128)(2,1)S(1)} %get-tuple-element.16.score_ref, bf16[3,64,128]{2,1,0:T(8,128)(2,1)S(1)} %get-tuple-element.17.value_ref), custom_call_target="tpu_custom_call" | custom-call | flops 12884901888 | bytes 4194304 | tf_op jit(solution)/shard_map/attend/pallas_call | solution.py:308
  37.7 7.9 %collective-permute-start.2 = (f32[2,72,128]{2,1,0:T(8,128)S(1)}, f32[2,72,128]{2,1,0:T(8,128)S(1)}, u32[]{:S(2)}, u32[]{:S(2)}) collective-permute-start(f32[2,72,128]{2,1,0:T(8,128)S(1)} %pad_maximum_fusion.3), channel_id=1, source_target_pairs={{0,128},{16,144},{32,160},{48,176},{64,192},{80,208},{96,224},{112... | collective-permute-start | bytes 221192 | tf_op jit(solution)/shard_map/ppermute | solution.py:304
  45.6 3.5 %all-to-all-start.1 = ((bf16[16,64,128]{2,1,0:T(8,128)(2,1)}), bf16[16,64,128]{2,1,0:T(8,128)(2,1)S(1)}, u32[]{:S(2)}, u32[]{:S(2)}) async-start(bf16[16,64,128]{2,1,0:T(8,128)(2,1)} %attend.1), calls=%async_computation.1 | async-start | bytes 524288 | tf_op jit(solution)/shard_map/all_to_all | solution.py:328
  49.1 0.0 collective-permute-done.2
  49.2 0.9 %collective-permute-start.3 = (f32[4,72,128]{2,1,0:T(8,128)S(1)}, f32[4,72,128]{2,1,0:T(8,128)S(1)}, u32[]{:S(2)}, u32[]{:S(2)}) collective-permute-start(f32[4,72,128]{2,1,0:T(8,128)S(1)} %pad_maximum_fusion.2), channel_id=1, source_target_pairs={{0,64},{16,80},{32,96},{48,112},{64,0},{80,16},{96,32},{112,48},{1... | collective-permute-start | bytes 442376 | tf_op jit(solution)/shard_map/ppermute | solution.py:304
  50.1 6.5 %all-to-all-done.1.shares_ref = bf16[16,64,128]{2,1,0:T(8,128)(2,1)S(1)} async-done(((bf16[16,64,128]{2,1,0:T(8,128)(2,1)}), bf16[16,64,128]{2,1,0:T(8,128)(2,1)S(1)}, u32[]{:S(2)}, u32[]{:S(2)}) %all-to-all-start.1) | async-done | bytes 262176 | tf_op jit(solution)/shard_map/all_to_all | solution.py:328
  56.6 0.9 predict.1
  57.5 7.2 %all-to-all-start.2 = ((bf16[16,64,128]{2,1,0:T(8,128)(2,1)}), bf16[16,64,128]{2,1,0:T(8,128)(2,1)S(1)}, u32[]{:S(2)}, u32[]{:S(2)}) async-start(bf16[16,64,128]{2,1,0:T(8,128)(2,1)} %predict.1), calls=%async_computation.2 | async-start | bytes 524288 | tf_op jit(solution)/shard_map/all_to_all | solution.py:339
  64.7 0.0 collective-permute-done.3
  64.8 0.2 collective-permute-start.4
  65.0 1.5 %collective-permute-done.4 = f32[8,72,128]{2,1,0:T(8,128)S(1)} collective-permute-done((f32[8,72,128]{2,1,0:T(8,128)S(1)}, f32[8,72,128]{2,1,0:T(8,128)S(1)}, u32[]{:S(2)}, u32[]{:S(2)}) %collective-permute-start.4) | collective-permute-done | bytes 294944 | tf_op jit(solution)/shard_map/ppermute | solution.py:304
  66.5 10.0 %all-to-all-done.2.pred_ref = bf16[16,64,128]{2,1,0:T(8,128)(2,1)S(1)} async-done(((bf16[16,64,128]{2,1,0:T(8,128)(2,1)}), bf16[16,64,128]{2,1,0:T(8,128)(2,1)S(1)}, u32[]{:S(2)}, u32[]{:S(2)}) %all-to-all-start.2) | async-done | bytes 262176 | tf_op jit(solution)/shard_map/all_to_all | solution.py:339
  76.4 0.8 prefix.1
  77.2 9.0 %all_to_all.20 = f32[16,1,128]{2,1,0:T(1,128)S(1)} all-to-all(f32[16,1,128]{2,1,0:T(1,128)S(1)} %get-tuple-element.25), channel_id=1, replica_groups=mesh['tm'=16,'head'=16] {'head'}, dimensions={0} | all-to-all | bytes 16384 | tf_op jit(solution)/shard_map/all_to_all | solution.py:351
  86.3 0.6 reduce_max.9
  (5 shorter events, 0.1 us)
Async XLA Ops:
  0.6 13.4 %collective-permute-start = (f32[3,1,3072]{2,1,0:T(1,128)}, f32[3,1,3072]{2,1,0:T(1,128)S(1)}, u32[]{:S(2)}, u32[]{:S(2)}) collective-permute-start(f32[3,1,3072]{2,1,0:T(1,128)} %bitcast.15), channel_id=1, source_target_pairs={{0,240},{16,0},{32,16},{48,32},{64,48},{80,64},{96,80},{112,96},{1... | collective-permute-start | bytes 110600 | tf_op jit(solution)/shard_map/ppermute | solution.py:270
  7.2 12.6 %all-to-all-start = ((bf16[16,64,128]{2,1,0:T(8,128)(2,1)}), bf16[16,64,128]{2,1,0:T(8,128)(2,1)S(1)}, u32[]{:S(2)}, u32[]{:S(2)}) async-start(bf16[16,64,128]{2,1,0:T(8,128)(2,1)} %get-tuple-element.14), calls=%async_computation | async-start | bytes 524288 | tf_op jit(solution)/shard_map/all_to_all | solution.py:271
  12.3 6.0 %collective-permute-start.1 = (f32[1,72,128]{2,1,0:T(8,128)S(1)}, f32[1,72,128]{2,1,0:T(8,128)S(1)}, u32[]{:S(2)}, u32[]{:S(2)}) collective-permute-start(f32[1,72,128]{2,1,0:T(8,128)S(1)} %get-tuple-element.18), channel_id=1, source_target_pairs={{0,32},{16,48},{32,0},{48,16},{64,96},{80,112},{96,64},{112,80},{1... | collective-permute-start | bytes 110600 | tf_op jit(solution)/shard_map/ppermute | solution.py:304
  37.7 11.4 %collective-permute-start.2 = (f32[2,72,128]{2,1,0:T(8,128)S(1)}, f32[2,72,128]{2,1,0:T(8,128)S(1)}, u32[]{:S(2)}, u32[]{:S(2)}) collective-permute-start(f32[2,72,128]{2,1,0:T(8,128)S(1)} %pad_maximum_fusion.3), channel_id=1, source_target_pairs={{0,128},{16,144},{32,160},{48,176},{64,192},{80,208},{96,224},{112... | collective-permute-start | bytes 221192 | tf_op jit(solution)/shard_map/ppermute | solution.py:304
  45.6 11.0 %all-to-all-start.1 = ((bf16[16,64,128]{2,1,0:T(8,128)(2,1)}), bf16[16,64,128]{2,1,0:T(8,128)(2,1)S(1)}, u32[]{:S(2)}, u32[]{:S(2)}) async-start(bf16[16,64,128]{2,1,0:T(8,128)(2,1)} %attend.1), calls=%async_computation.1 | async-start | bytes 524288 | tf_op jit(solution)/shard_map/all_to_all | solution.py:328
  49.2 15.6 %collective-permute-start.3 = (f32[4,72,128]{2,1,0:T(8,128)S(1)}, f32[4,72,128]{2,1,0:T(8,128)S(1)}, u32[]{:S(2)}, u32[]{:S(2)}) collective-permute-start(f32[4,72,128]{2,1,0:T(8,128)S(1)} %pad_maximum_fusion.2), channel_id=1, source_target_pairs={{0,64},{16,80},{32,96},{48,112},{64,0},{80,16},{96,32},{112,48},{1... | collective-permute-start | bytes 442376 | tf_op jit(solution)/shard_map/ppermute | solution.py:304
  57.5 18.9 %all-to-all-start.2 = ((bf16[16,64,128]{2,1,0:T(8,128)(2,1)}), bf16[16,64,128]{2,1,0:T(8,128)(2,1)S(1)}, u32[]{:S(2)}, u32[]{:S(2)}) async-start(bf16[16,64,128]{2,1,0:T(8,128)(2,1)} %predict.1), calls=%async_computation.2 | async-start | bytes 524288 | tf_op jit(solution)/shard_map/all_to_all | solution.py:339
  64.8 1.7 %collective-permute-start.4 = (f32[8,72,128]{2,1,0:T(8,128)S(1)}, f32[8,72,128]{2,1,0:T(8,128)S(1)}, u32[]{:S(2)}, u32[]{:S(2)}) collective-permute-start(f32[8,72,128]{2,1,0:T(8,128)S(1)} %pad_maximum_fusion.1), channel_id=1, source_target_pairs={{0,16},{16,0},{32,48},{48,32},{64,80},{80,64},{96,112},{112,96},{1... | collective-permute-start | bytes 884744 | tf_op jit(solution)/shard_map/ppermute | solution.py:304

commit v4 on v3

--- a/solution.py
+++ b/solution.py
@@ -96,24 +96,31 @@
         value_ref[h] = value.astype(BF16)
 
 
+def latents_kernel(steps_ref, lat_ref, table_ref, pay_ref):
+    table = table_ref[...]
+    picked = jnp.where(lane_ids(table.shape) == steps_ref[0], table, 0.0)
+    coefs = jnp.broadcast_to(jnp.sum(picked, -1, keepdims=True), (2, LANES))
+    pay_ref[0] = jnp.concatenate([lat_ref[...]] + [coefs] * 4, 0)
+
+
 def tokens_kernel(
-    last_ref, steps_hbm, lat_hbm, table_hbm, w_in_hbm, start_hbm,
-    pay_ref, cur_ref, lat_ref, w_in_ref, start_ref, own_ref, table_ref, steps_ref, sems,
+    lat_hbm, w_in_hbm, start_hbm, table_hbm,
+    pay_ref, cur_ref, w_in_ref, start_ref, lat_ref, table_ref, own_ref, sems,
 ):
     moves = [
-        (lat_hbm, lat_ref.at[0, pl.ds(0, HD)]),
+        (lat_hbm, lat_ref),
         (start_hbm, start_ref),
         (w_in_hbm, w_in_ref),
-        (steps_hbm, steps_ref),
         (table_hbm, table_ref),
     ]
     parts = pay_ref.shape[0]
     copies = [pltpu.make_async_copy(a, b, sems.at[parts + i]) for i, (a, b) in enumerate(moves)]
     for copy in copies:
         copy.start()
-    for copy in copies[:3]:
+    for copy in copies:
         copy.wait()
-    current_t = jnp.where(last_ref[0] == 1, start_ref[...], lat_ref[0, :HD])
+    last = lax.axis_index("tm") == lax.axis_size("tm") - 1
+    current_t = jnp.where(last, start_ref[...], lat_ref[...])
     cur_ref[...] = current_t
     rounded = jnp.transpose(current_t).astype(BF16)
     hidden = jnp.dot(rounded, w_in_ref[...], preferred_element_type=F32)
@@ -124,12 +131,6 @@
     sends = [pltpu.make_async_copy(own_ref, pay_ref.at[i], sems.at[i]) for i in range(parts)]
     for send in sends:
         send.start()
-    for copy in copies[3:]:
-        copy.wait()
-    table = table_ref[...]
-    picked = jnp.where(lane_ids(table.shape) == steps_ref[0], table, 0.0)
-    coefs = jnp.broadcast_to(jnp.sum(picked, -1, keepdims=True), (2, LANES))
-    lat_ref[0, pl.ds(HD, 8)] = jnp.concatenate([coefs] * 4, 0)
     for send in sends:
         send.wait()
 
@@ -195,7 +196,8 @@
     return (i & 1) * 8 + (i & 4) + ((i & 8) >> 2) + ((i & 2) >> 1)
 
 
-def prefix_kernel(pos_ref, pred_ref, lat_ref, start_ref, out_ref, err_ref):
+def prefix_kernel(pred_ref, lat_ref, start_ref, out_ref, err_ref):
+    pos = lax.axis_index("tm")
     window = pred_ref.shape[0]
     start = start_ref[...]
     refreshed = start
@@ -204,7 +206,7 @@
     errors = jnp.zeros((1, LANES), F32)
     lanes = lane_ids((1, LANES))
     for s in range(window):
-        at = jnp.bitwise_xor(mirrored(pos_ref[0]), mirrored(s))
+        at = jnp.bitwise_xor(mirrored(pos), mirrored(s))
         predicted = pred_ref[(s - 1) % window].astype(F32)
         c0, c1 = lat_ref[at, HD : HD + 1], lat_ref[at, HD + 1 : HD + 2]
         refreshed += c0 * current + c1 * predicted
@@ -212,7 +214,7 @@
         difference = refreshed - current
         error = jnp.sum(difference * difference, axis=(0, 1), keepdims=True)
         errors += jnp.where(lanes == s, error, 0.0)
-        own = jnp.where(pos_ref[0] == s, refreshed, own)
+        own = jnp.where(pos == s, refreshed, own)
     out_ref[...] = own
     for i in range(err_ref.shape[0]):
         err_ref[i] = errors
@@ -238,7 +240,6 @@
     units = w_qkv.shape[1]
     local_heads = units // HD
     seq = groups * own_rows
-    pos = lax.axis_index("tm").astype(jnp.int32).reshape(1)
     start_t = start.T
     lat_t = latents[0].T
     table_t = ddim_table.T
@@ -246,27 +247,33 @@
 
     in_hbm = lambda x: pltpu.with_memory_space_constraint(x, pltpu.HBM)
     hbm = pl.BlockSpec(memory_space=pltpu.HBM)
-    last = (pos == window - 1).astype(jnp.int32)
-    pay, cur_t, lat_pay, w_in_near, start_near = pl.pallas_call(
+    pay, cur_t, w_in_near, start_near, lat_near, table_near = pl.pallas_call(
         tokens_kernel,
-        in_specs=[smem(), pl.BlockSpec(memory_space=pl.ANY), hbm, hbm, hbm, hbm],
-        out_specs=[hbm] + [vmem()] * 4,
+        in_specs=[hbm] * 4,
+        out_specs=[hbm] + [vmem()] * 5,
         out_shape=[
             pltpu.HBM((groups, HD, own_rows), BF16),
             pltpu.VMEM((HD, own_rows), F32),
-            pltpu.VMEM((1, HD + 8, own_rows), F32),
             pltpu.VMEM((HD, d), BF16),
             pltpu.VMEM((HD, own_rows), F32),
+            pltpu.VMEM((HD, own_rows), F32),
+            pltpu.VMEM((2, ddim_table.shape[0]), F32),
         ],
         scratch_shapes=[
             pltpu.VMEM((HD, own_rows), BF16),
-            pltpu.VMEM((2, ddim_table.shape[0]), F32),
-            pltpu.SMEM((1,), jnp.int32),
-            pltpu.SemaphoreType.DMA((groups + 5,)),
+            pltpu.SemaphoreType.DMA((groups + 4,)),
         ],
         compiler_params=params_of(8),
         name="tokens",
-    )(last, steps_window, in_hbm(lat_t), in_hbm(table_t), in_hbm(w_in), in_hbm(start_t))
+    )(in_hbm(lat_t), in_hbm(w_in), in_hbm(start_t), in_hbm(table_t))
+    lat_pay = pl.pallas_call(
+        latents_kernel,
+        in_specs=[smem(), vmem(), vmem()],
+        out_specs=vmem(),
+        out_shape=pltpu.VMEM((1, HD + 8, own_rows), F32),
+        compiler_params=params_of(8),
+        name="latents",
+    )(steps_window, lat_near, table_near)
     mod = lax.ppermute(mod, "tm", [(i, (i - 1) % window) for i in range(window)])
     tokens = lax.all_to_all(pay, "head", 0, 0, tiled=True)
 
@@ -339,7 +346,7 @@
     pred_all = lax.all_to_all(pred_pay, "tm", 0, 0, tiled=True)
     refreshed_t, err_pay = pl.pallas_call(
         prefix_kernel,
-        in_specs=[smem(), vmem(), vmem(), vmem()],
+        in_specs=[vmem(), vmem(), vmem()],
         out_specs=[vmem(), vmem()],
         out_shape=[
             jax.ShapeDtypeStruct((HD, own_rows), F32),
@@ -347,7 +354,7 @@
         ],
         compiler_params=params_of(32),
         name="prefix",
-    )(pos, pred_all, lat_all, start_near)
+    )(pred_all, lat_all, start_near)
     errors = lax.all_to_all(err_pay, "head", 0, 0, tiled=True)
     worst = jnp.max(jnp.sum(errors, axis=(0, 1)))
     return refreshed_t.T[None], worst / (seq * HD)

time: 89.2 us -> 89.2 us (level)
  waiting for transfers between devices: 19.5 us -> 18.6 us
    pallas_call x2 -> x3, Pallas kernels: 3.47 us -> 3.56 us  [the longest x1 2.69 us: on_device(): pl.pallas_call(tokens_kernel, in_specs=[hbm] * 4, out_specs=[hbm] + [vmem...]
where the time goes in v4:
time: 89.2 us; the launch traced here: 88.7 us
  starting transfers between devices  30.6 us (34%)
  Pallas kernels  26.6 us (30%)
  waiting for transfers between devices  18.6 us (21%)
  blocking collectives  9.01 us (10%)
  between operations  3.14 us (4%)
    pallas_call x1, Pallas kernels, on_device(): pl.pallas_call(functools.partial(attend_kernel, span=seq), in_specs=[vmem...  17.9 us
    ppermute x4, starting transfers between devices, spread(): other = lax.ppermute(entries, 'tm', [(i, i ^ by) for i in range(window)])  11 us
    all_to_all x1, waiting for transfers between devices, on_device(): pred_all = lax.all_to_all(pred_pay, 'tm', 0, 0, tiled=True)  9.96 us
    all_to_all x1, blocking collectives, on_device(): errors = lax.all_to_all(err_pay, 'head', 0, 0, tiled=True)  9.01 us
    all_to_all x1, starting transfers between devices, on_device(): pred_all = lax.all_to_all(pred_pay, 'tm', 0, 0, tiled=True)  7.35 us
    all_to_all x1, waiting for transfers between devices, on_device(): shares = lax.all_to_all(shares, 'head', 0, 0, tiled=True)  6.29 us
    all_to_all x1, starting transfers between devices, on_device(): tokens = lax.all_to_all(pay, 'head', 0, 0, tiled=True)  5.03 us
    pallas_call x1, Pallas kernels, on_device(): pl.pallas_call(weights_kernel, in_specs=[vmem(), vmem(), hbm, hbm, hbm],...  4.28 us
  transfers between devices with their start and end apart: 8, of which 4 were waited for; matrix products, arithmetic and copies ran while one was open for 0% of the time, Pallas kernels for 9%

profile of v4, /device:TPU:1, one launch (start us, length us, event | category | flops | bytes accessed | tf_op | source)
XLA Modules:
  0.0 88.7 jit_solution(5453052604058171746)
XLA Ops:
  0.6 3.3 %collective-permute-start = (f32[3,1,3072]{2,1,0:T(1,128)}, f32[3,1,3072]{2,1,0:T(1,128)S(1)}, u32[]{:S(2)}, u32[]{:S(2)}) collective-permute-start(f32[3,1,3072]{2,1,0:T(1,128)} %bitcast.14), channel_id=1, source_target_pairs={{0,240},{16,0},{32,16},{48,32},{64,48},{80,64},{96,80},{112,96},{1... | collective-permute-start | bytes 110600 | tf_op jit(solution)/shard_map/ppermute | solution.py:277
  3.9 2.7 %tokens.1 = (bf16[16,64,128]{2,1,0:T(8,128)(2,1)}, f32[64,128]{1,0:T(8,128)S(1)}, bf16[64,3072]{1,0:T(8,128)(2,1)S(1)}, f32[64,128]{1,0:T(8,128)S(1)}, f32[64,128]{1,0:T(8,128)S(1)}, /*index=5*/f32[2,1000]{1,0:T(2,128)S(1)}) custom-call(f32[64,128]{1,0:T(8,128)} %bitcast.11, bf16[64,3072]{1,0:T(8,128)(2,1)} %w_in_hbm.1, f32[64,128]{1,0:T(8,128)} %bitcast.12, ...), custom_call_target="tpu_custom_call" | custom-call | tf_op jit(solution)/shard_map/tokens/pallas_call | solution.py:250
  6.6 5.0 %all-to-all-start = ((bf16[16,64,128]{2,1,0:T(8,128)(2,1)}), bf16[16,64,128]{2,1,0:T(8,128)(2,1)S(1)}, u32[]{:S(2)}, u32[]{:S(2)}) async-start(bf16[16,64,128]{2,1,0:T(8,128)(2,1)} %get-tuple-element.15), calls=%async_computation | async-start | bytes 524288 | tf_op jit(solution)/shard_map/all_to_all | solution.py:278
  12.3 0.1 latents.1
  12.4 1.6 %collective-permute-start.1 = (f32[1,72,128]{2,1,0:T(8,128)S(1)}, f32[1,72,128]{2,1,0:T(8,128)S(1)}, u32[]{:S(2)}, u32[]{:S(2)}) collective-permute-start(f32[1,72,128]{2,1,0:T(8,128)S(1)} %latents.1), channel_id=1, source_target_pairs={{0,32},{16,48},{32,0},{48,16},{64,96},{80,112},{96,64},{112,80},{1... | collective-permute-start | bytes 110600 | tf_op jit(solution)/shard_map/ppermute | solution.py:311
  14.0 0.0 collective-permute-done.mod_ref
  14.0 4.3 %weights.1 = (bf16[3,128,128]{2,1,0:T(8,128)(2,1)S(1)}, bf16[3,64,128]{2,1,0:T(8,128)(2,1)S(1)}, f32[64,64]{1,0:T(8,128)S(1)}) custom-call(f32[3,1,3072]{2,1,0:T(1,128)S(1)} %collective-permute-done.mod_ref, bf16[64,3072]{1,0:T(8,128)(2,1)S(1)} %get-tuple-element.16.w_in_ref, bf16[3,192,3072]{2,1,0:T(8,128)(2,1)} %w_qkv_hbm.1, bf16[192,3072]{1,0:T(8,128)(2,1)} %w_out_hbm.1, ...), custom_call_target="tpu_custom_call" | custom-call | flops 1207959552 | bytes 4718592 | tf_op jit(solution)/shard_map/weights/pallas_call | solution.py:280
  18.3 0.0 collective-permute-done.1
  18.3 0.8 all-to-all-done.all_ref
  19.2 17.9 %attend.1 = bf16[16,64,128]{2,1,0:T(8,128)(2,1)} custom-call(bf16[16,64,128]{2,1,0:T(8,128)(2,1)S(1)} %all-to-all-done.all_ref, bf16[3,128,128]{2,1,0:T(8,128)(2,1)S(1)} %get-tuple-element.17.score_ref, bf16[3,64,128]{2,1,0:T(8,128)(2,1)S(1)} %get-tuple-element.18.value_ref), custom_call_target="tpu_custom_call" | custom-call | flops 12884901888 | bytes 4194304 | tf_op jit(solution)/shard_map/attend/pallas_call | solution.py:315
  37.1 7.9 %collective-permute-start.2 = (f32[2,72,128]{2,1,0:T(8,128)S(1)}, f32[2,72,128]{2,1,0:T(8,128)S(1)}, u32[]{:S(2)}, u32[]{:S(2)}) collective-permute-start(f32[2,72,128]{2,1,0:T(8,128)S(1)} %pad_maximum_fusion.3), channel_id=1, source_target_pairs={{0,128},{16,144},{32,160},{48,176},{64,192},{80,208},{96,224},{112... | collective-permute-start | bytes 221192 | tf_op jit(solution)/shard_map/ppermute | solution.py:311
  44.9 4.0 %all-to-all-start.1 = ((bf16[16,64,128]{2,1,0:T(8,128)(2,1)}), bf16[16,64,128]{2,1,0:T(8,128)(2,1)S(1)}, u32[]{:S(2)}, u32[]{:S(2)}) async-start(bf16[16,64,128]{2,1,0:T(8,128)(2,1)} %attend.1), calls=%async_computation.1 | async-start | bytes 524288 | tf_op jit(solution)/shard_map/all_to_all | solution.py:335
  48.9 0.0 collective-permute-done.2
  48.9 1.3 %collective-permute-start.3 = (f32[4,72,128]{2,1,0:T(8,128)S(1)}, f32[4,72,128]{2,1,0:T(8,128)S(1)}, u32[]{:S(2)}, u32[]{:S(2)}) collective-permute-start(f32[4,72,128]{2,1,0:T(8,128)S(1)} %pad_maximum_fusion.2), channel_id=1, source_target_pairs={{0,64},{16,80},{32,96},{48,112},{64,0},{80,16},{96,32},{112,48},{1... | collective-permute-start | bytes 442376 | tf_op jit(solution)/shard_map/ppermute | solution.py:311
  50.2 6.3 %all-to-all-done.1.shares_ref = bf16[16,64,128]{2,1,0:T(8,128)(2,1)S(1)} async-done(((bf16[16,64,128]{2,1,0:T(8,128)(2,1)}), bf16[16,64,128]{2,1,0:T(8,128)(2,1)S(1)}, u32[]{:S(2)}, u32[]{:S(2)}) %all-to-all-start.1) | async-done | bytes 262176 | tf_op jit(solution)/shard_map/all_to_all | solution.py:335
  56.5 0.9 predict.1
  57.4 7.3 %all-to-all-start.2 = ((bf16[16,64,128]{2,1,0:T(8,128)(2,1)}), bf16[16,64,128]{2,1,0:T(8,128)(2,1)S(1)}, u32[]{:S(2)}, u32[]{:S(2)}) async-start(bf16[16,64,128]{2,1,0:T(8,128)(2,1)} %predict.1), calls=%async_computation.2 | async-start | bytes 524288 | tf_op jit(solution)/shard_map/all_to_all | solution.py:346
  64.7 0.0 collective-permute-done.3
  64.8 0.2 collective-permute-start.4
  65.0 1.5 %collective-permute-done.4 = f32[8,72,128]{2,1,0:T(8,128)S(1)} collective-permute-done((f32[8,72,128]{2,1,0:T(8,128)S(1)}, f32[8,72,128]{2,1,0:T(8,128)S(1)}, u32[]{:S(2)}, u32[]{:S(2)}) %collective-permute-start.4) | collective-permute-done | bytes 294944 | tf_op jit(solution)/shard_map/ppermute | solution.py:311
  66.5 10.0 %all-to-all-done.2.pred_ref = bf16[16,64,128]{2,1,0:T(8,128)(2,1)S(1)} async-done(((bf16[16,64,128]{2,1,0:T(8,128)(2,1)}), bf16[16,64,128]{2,1,0:T(8,128)(2,1)S(1)}, u32[]{:S(2)}, u32[]{:S(2)}) %all-to-all-start.2) | async-done | bytes 262176 | tf_op jit(solution)/shard_map/all_to_all | solution.py:346
  76.4 0.8 prefix.1
  77.2 9.0 %all_to_all.20 = f32[16,1,128]{2,1,0:T(1,128)S(1)} all-to-all(f32[16,1,128]{2,1,0:T(1,128)S(1)} %get-tuple-element.27), channel_id=1, replica_groups=mesh['tm'=16,'head'=16] {'head'}, dimensions={0} | all-to-all | bytes 16384 | tf_op jit(solution)/shard_map/all_to_all | solution.py:358
  86.3 0.6 reduce_max.9
  (5 shorter events, 0.1 us)
Async XLA Ops:
  0.6 13.4 %collective-permute-start = (f32[3,1,3072]{2,1,0:T(1,128)}, f32[3,1,3072]{2,1,0:T(1,128)S(1)}, u32[]{:S(2)}, u32[]{:S(2)}) collective-permute-start(f32[3,1,3072]{2,1,0:T(1,128)} %bitcast.14), channel_id=1, source_target_pairs={{0,240},{16,0},{32,16},{48,32},{64,48},{80,64},{96,80},{112,96},{1... | collective-permute-start | bytes 110600 | tf_op jit(solution)/shard_map/ppermute | solution.py:277
  6.6 12.6 %all-to-all-start = ((bf16[16,64,128]{2,1,0:T(8,128)(2,1)}), bf16[16,64,128]{2,1,0:T(8,128)(2,1)S(1)}, u32[]{:S(2)}, u32[]{:S(2)}) async-start(bf16[16,64,128]{2,1,0:T(8,128)(2,1)} %get-tuple-element.15), calls=%async_computation | async-start | bytes 524288 | tf_op jit(solution)/shard_map/all_to_all | solution.py:278
  12.4 5.9 %collective-permute-start.1 = (f32[1,72,128]{2,1,0:T(8,128)S(1)}, f32[1,72,128]{2,1,0:T(8,128)S(1)}, u32[]{:S(2)}, u32[]{:S(2)}) collective-permute-start(f32[1,72,128]{2,1,0:T(8,128)S(1)} %latents.1), channel_id=1, source_target_pairs={{0,32},{16,48},{32,0},{48,16},{64,96},{80,112},{96,64},{112,80},{1... | collective-permute-start | bytes 110600 | tf_op jit(solution)/shard_map/ppermute | solution.py:311
  37.1 11.8 %collective-permute-start.2 = (f32[2,72,128]{2,1,0:T(8,128)S(1)}, f32[2,72,128]{2,1,0:T(8,128)S(1)}, u32[]{:S(2)}, u32[]{:S(2)}) collective-permute-start(f32[2,72,128]{2,1,0:T(8,128)S(1)} %pad_maximum_fusion.3), channel_id=1, source_target_pairs={{0,128},{16,144},{32,160},{48,176},{64,192},{80,208},{96,224},{112... | collective-permute-start | bytes 221192 | tf_op jit(solution)/shard_map/ppermute | solution.py:311
  44.9 11.6 %all-to-all-start.1 = ((bf16[16,64,128]{2,1,0:T(8,128)(2,1)}), bf16[16,64,128]{2,1,0:T(8,128)(2,1)S(1)}, u32[]{:S(2)}, u32[]{:S(2)}) async-start(bf16[16,64,128]{2,1,0:T(8,128)(2,1)} %attend.1), calls=%async_computation.1 | async-start | bytes 524288 | tf_op jit(solution)/shard_map/all_to_all | solution.py:335
  48.9 15.8 %collective-permute-start.3 = (f32[4,72,128]{2,1,0:T(8,128)S(1)}, f32[4,72,128]{2,1,0:T(8,128)S(1)}, u32[]{:S(2)}, u32[]{:S(2)}) collective-permute-start(f32[4,72,128]{2,1,0:T(8,128)S(1)} %pad_maximum_fusion.2), channel_id=1, source_target_pairs={{0,64},{16,80},{32,96},{48,112},{64,0},{80,16},{96,32},{112,48},{1... | collective-permute-start | bytes 442376 | tf_op jit(solution)/shard_map/ppermute | solution.py:311
  57.4 19.1 %all-to-all-start.2 = ((bf16[16,64,128]{2,1,0:T(8,128)(2,1)}), bf16[16,64,128]{2,1,0:T(8,128)(2,1)S(1)}, u32[]{:S(2)}, u32[]{:S(2)}) async-start(bf16[16,64,128]{2,1,0:T(8,128)(2,1)} %predict.1), calls=%async_computation.2 | async-start | bytes 524288 | tf_op jit(solution)/shard_map/all_to_all | solution.py:346
  64.8 1.7 %collective-permute-start.4 = (f32[8,72,128]{2,1,0:T(8,128)S(1)}, f32[8,72,128]{2,1,0:T(8,128)S(1)}, u32[]{:S(2)}, u32[]{:S(2)}) collective-permute-start(f32[8,72,128]{2,1,0:T(8,128)S(1)} %pad_maximum_fusion.1), channel_id=1, source_target_pairs={{0,16},{16,0},{32,48},{48,32},{64,80},{80,64},{96,112},{112,96},{1... | collective-permute-start | bytes 884744 | tf_op jit(solution)/shard_map/ppermute | solution.py:311

commit v5 on v3

--- a/solution.py
+++ b/solution.py
@@ -152,8 +152,8 @@
 
     query_norm = 0.0
     for h in range(heads):
-        columns = jnp.dot(score_ref[h], keys_t[...], preferred_element_type=F32).astype(BF16)
-        queries[h] = columns
+        columns = jnp.dot(score_ref[h], keys_t[...], preferred_element_type=F32)
+        queries[h] = columns.astype(BF16)
         query_norm = jnp.maximum(query_norm, longest(columns))
     safe = query_norm * longest(keys_t[...]) <= SAFE * SAFE
     sums[...] = jnp.zeros_like(sums)

time: 89.2 us -> 89.1 us (level)
  no operation moved by 1% of the time
where the time goes in v5:
time: 89.1 us; the launch traced here: 88.5 us
  starting transfers between devices  29.8 us (33%)
  Pallas kernels  26.4 us (30%)
  waiting for transfers between devices  19.5 us (22%)
  blocking collectives  9.02 us (10%)
  between operations  3.14 us (4%)
    pallas_call x1, Pallas kernels, on_device(): pl.pallas_call(functools.partial(attend_kernel, span=seq), in_specs=[vmem...  17.8 us
    ppermute x4, starting transfers between devices, spread(): other = lax.ppermute(entries, 'tm', [(i, i ^ by) for i in range(window)])  10.8 us
    all_to_all x1, waiting for transfers between devices, on_device(): pred_all = lax.all_to_all(pred_pay, 'tm', 0, 0, tiled=True)  9.96 us
    all_to_all x1, blocking collectives, on_device(): errors = lax.all_to_all(err_pay, 'head', 0, 0, tiled=True)  9.02 us
    all_to_all x1, starting transfers between devices, on_device(): pred_all = lax.all_to_all(pred_pay, 'tm', 0, 0, tiled=True)  7.21 us
    all_to_all x1, waiting for transfers between devices, on_device(): shares = lax.all_to_all(shares, 'head', 0, 0, tiled=True)  6.51 us
    all_to_all x1, starting transfers between devices, on_device(): tokens = lax.all_to_all(pay, 'head', 0, 0, tiled=True)  5.03 us
    pallas_call x1, Pallas kernels, on_device(): pl.pallas_call(weights_kernel, in_specs=[vmem(), vmem(), hbm, hbm, hbm],...  4.28 us
  transfers between devices with their start and end apart: 8, of which 4 were waited for; matrix products, arithmetic and copies ran while one was open for 0% of the time, Pallas kernels for 9%

profile of v5, /device:TPU:1, one launch (start us, length us, event | category | flops | bytes accessed | tf_op | source)
XLA Modules:
  0.0 88.5 jit_solution(16122689281284220943)
XLA Ops:
  0.6 3.3 %collective-permute-start = (f32[3,1,3072]{2,1,0:T(1,128)}, f32[3,1,3072]{2,1,0:T(1,128)S(1)}, u32[]{:S(2)}, u32[]{:S(2)}) collective-permute-start(f32[3,1,3072]{2,1,0:T(1,128)} %bitcast.15), channel_id=1, source_target_pairs={{0,240},{16,0},{32,16},{48,32},{64,48},{80,64},{96,80},{112,96},{1... | collective-permute-start | bytes 110600 | tf_op jit(solution)/shard_map/ppermute | solution.py:270
  4.5 2.7 %tokens.1 = (bf16[16,64,128]{2,1,0:T(8,128)(2,1)}, f32[64,128]{1,0:T(8,128)S(1)}, f32[1,72,128]{2,1,0:T(8,128)S(1)}, bf16[64,3072]{1,0:T(8,128)(2,1)S(1)}, f32[64,128]{1,0:T(8,128)S(1)}) custom-call(s32[1]{0:T(128)S(6)} %convert_element_type.3.last_ref, s32[1]{0:T(128)S(6)} %copy.11.steps_hbm, f32[64,128]{1,0:T(8,128)} %bitcast.12, f32[2,1000]{1,0:T(2,128)} %bitcast.14, ...), custom_call_target="tpu_custom_call" | custom-call | tf_op jit(solution)/shard_map/tokens/pallas_call | solution.py:250
  7.2 5.0 %all-to-all-start = ((bf16[16,64,128]{2,1,0:T(8,128)(2,1)}), bf16[16,64,128]{2,1,0:T(8,128)(2,1)S(1)}, u32[]{:S(2)}, u32[]{:S(2)}) async-start(bf16[16,64,128]{2,1,0:T(8,128)(2,1)} %get-tuple-element.14), calls=%async_computation | async-start | bytes 524288 | tf_op jit(solution)/shard_map/all_to_all | solution.py:271
  12.3 1.7 %collective-permute-start.1 = (f32[1,72,128]{2,1,0:T(8,128)S(1)}, f32[1,72,128]{2,1,0:T(8,128)S(1)}, u32[]{:S(2)}, u32[]{:S(2)}) collective-permute-start(f32[1,72,128]{2,1,0:T(8,128)S(1)} %get-tuple-element.18), channel_id=1, source_target_pairs={{0,32},{16,48},{32,0},{48,16},{64,96},{80,112},{96,64},{112,80},{1... | collective-permute-start | bytes 110600 | tf_op jit(solution)/shard_map/ppermute | solution.py:304
  14.0 0.0 collective-permute-done.mod_ref
  14.0 4.3 %weights.1 = (bf16[3,128,128]{2,1,0:T(8,128)(2,1)S(1)}, bf16[3,64,128]{2,1,0:T(8,128)(2,1)S(1)}, f32[64,64]{1,0:T(8,128)S(1)}) custom-call(f32[3,1,3072]{2,1,0:T(1,128)S(1)} %collective-permute-done.mod_ref, bf16[64,3072]{1,0:T(8,128)(2,1)S(1)} %get-tuple-element.15.w_in_ref, bf16[3,192,3072]{2,1,0:T(8,128)(2,1)} %w_qkv_hbm.1, bf16[192,3072]{1,0:T(8,128)(2,1)} %w_out_hbm.1, ...), custom_call_target="tpu_custom_call" | custom-call | flops 1207959552 | bytes 4718592 | tf_op jit(solution)/shard_map/weights/pallas_call | solution.py:273
  18.3 0.0 collective-permute-done.1
  18.3 1.5 %all-to-all-done.all_ref = bf16[16,64,128]{2,1,0:T(8,128)(2,1)S(1)} async-done(((bf16[16,64,128]{2,1,0:T(8,128)(2,1)}), bf16[16,64,128]{2,1,0:T(8,128)(2,1)S(1)}, u32[]{:S(2)}, u32[]{:S(2)}) %all-to-all-start) | async-done | bytes 262176 | tf_op jit(solution)/shard_map/all_to_all | solution.py:271
  19.8 17.8 %attend.1 = bf16[16,64,128]{2,1,0:T(8,128)(2,1)} custom-call(bf16[16,64,128]{2,1,0:T(8,128)(2,1)S(1)} %all-to-all-done.all_ref, bf16[3,128,128]{2,1,0:T(8,128)(2,1)S(1)} %get-tuple-element.16.score_ref, bf16[3,64,128]{2,1,0:T(8,128)(2,1)S(1)} %get-tuple-element.17.value_ref), custom_call_target="tpu_custom_call" | custom-call | flops 12884901888 | bytes 4194304 | tf_op jit(solution)/shard_map/attend/pallas_call | solution.py:308
  37.6 7.9 %collective-permute-start.2 = (f32[2,72,128]{2,1,0:T(8,128)S(1)}, f32[2,72,128]{2,1,0:T(8,128)S(1)}, u32[]{:S(2)}, u32[]{:S(2)}) collective-permute-start(f32[2,72,128]{2,1,0:T(8,128)S(1)} %pad_maximum_fusion.3), channel_id=1, source_target_pairs={{0,128},{16,144},{32,160},{48,176},{64,192},{80,208},{96,224},{112... | collective-permute-start | bytes 221192 | tf_op jit(solution)/shard_map/ppermute | solution.py:304
  45.5 3.5 %all-to-all-start.1 = ((bf16[16,64,128]{2,1,0:T(8,128)(2,1)}), bf16[16,64,128]{2,1,0:T(8,128)(2,1)S(1)}, u32[]{:S(2)}, u32[]{:S(2)}) async-start(bf16[16,64,128]{2,1,0:T(8,128)(2,1)} %attend.1), calls=%async_computation.1 | async-start | bytes 524288 | tf_op jit(solution)/shard_map/all_to_all | solution.py:328
  49.0 0.0 collective-permute-done.2
  49.0 1.0 %collective-permute-start.3 = (f32[4,72,128]{2,1,0:T(8,128)S(1)}, f32[4,72,128]{2,1,0:T(8,128)S(1)}, u32[]{:S(2)}, u32[]{:S(2)}) collective-permute-start(f32[4,72,128]{2,1,0:T(8,128)S(1)} %pad_maximum_fusion.2), channel_id=1, source_target_pairs={{0,64},{16,80},{32,96},{48,112},{64,0},{80,16},{96,32},{112,48},{1... | collective-permute-start | bytes 442376 | tf_op jit(solution)/shard_map/ppermute | solution.py:304
  50.0 6.5 %all-to-all-done.1.shares_ref = bf16[16,64,128]{2,1,0:T(8,128)(2,1)S(1)} async-done(((bf16[16,64,128]{2,1,0:T(8,128)(2,1)}), bf16[16,64,128]{2,1,0:T(8,128)(2,1)S(1)}, u32[]{:S(2)}, u32[]{:S(2)}) %all-to-all-start.1) | async-done | bytes 262176 | tf_op jit(solution)/shard_map/all_to_all | solution.py:328
  56.5 0.9 predict.1
  57.4 7.2 %all-to-all-start.2 = ((bf16[16,64,128]{2,1,0:T(8,128)(2,1)}), bf16[16,64,128]{2,1,0:T(8,128)(2,1)S(1)}, u32[]{:S(2)}, u32[]{:S(2)}) async-start(bf16[16,64,128]{2,1,0:T(8,128)(2,1)} %predict.1), calls=%async_computation.2 | async-start | bytes 524288 | tf_op jit(solution)/shard_map/all_to_all | solution.py:339
  64.6 0.0 collective-permute-done.3
  64.6 0.2 collective-permute-start.4
  64.8 1.5 %collective-permute-done.4 = f32[8,72,128]{2,1,0:T(8,128)S(1)} collective-permute-done((f32[8,72,128]{2,1,0:T(8,128)S(1)}, f32[8,72,128]{2,1,0:T(8,128)S(1)}, u32[]{:S(2)}, u32[]{:S(2)}) %collective-permute-start.4) | collective-permute-done | bytes 294944 | tf_op jit(solution)/shard_map/ppermute | solution.py:304
  66.3 10.0 %all-to-all-done.2.pred_ref = bf16[16,64,128]{2,1,0:T(8,128)(2,1)S(1)} async-done(((bf16[16,64,128]{2,1,0:T(8,128)(2,1)}), bf16[16,64,128]{2,1,0:T(8,128)(2,1)S(1)}, u32[]{:S(2)}, u32[]{:S(2)}) %all-to-all-start.2) | async-done | bytes 262176 | tf_op jit(solution)/shard_map/all_to_all | solution.py:339
  76.3 0.8 prefix.1
  77.1 9.0 %all_to_all.20 = f32[16,1,128]{2,1,0:T(1,128)S(1)} all-to-all(f32[16,1,128]{2,1,0:T(1,128)S(1)} %get-tuple-element.25), channel_id=1, replica_groups=mesh['tm'=16,'head'=16] {'head'}, dimensions={0} | all-to-all | bytes 16384 | tf_op jit(solution)/shard_map/all_to_all | solution.py:351
  86.1 0.6 reduce_max.9
  (5 shorter events, 0.1 us)
Async XLA Ops:
  0.6 13.4 %collective-permute-start = (f32[3,1,3072]{2,1,0:T(1,128)}, f32[3,1,3072]{2,1,0:T(1,128)S(1)}, u32[]{:S(2)}, u32[]{:S(2)}) collective-permute-start(f32[3,1,3072]{2,1,0:T(1,128)} %bitcast.15), channel_id=1, source_target_pairs={{0,240},{16,0},{32,16},{48,32},{64,48},{80,64},{96,80},{112,96},{1... | collective-permute-start | bytes 110600 | tf_op jit(solution)/shard_map/ppermute | solution.py:270
  7.2 12.6 %all-to-all-start = ((bf16[16,64,128]{2,1,0:T(8,128)(2,1)}), bf16[16,64,128]{2,1,0:T(8,128)(2,1)S(1)}, u32[]{:S(2)}, u32[]{:S(2)}) async-start(bf16[16,64,128]{2,1,0:T(8,128)(2,1)} %get-tuple-element.14), calls=%async_computation | async-start | bytes 524288 | tf_op jit(solution)/shard_map/all_to_all | solution.py:271
  12.3 6.0 %collective-permute-start.1 = (f32[1,72,128]{2,1,0:T(8,128)S(1)}, f32[1,72,128]{2,1,0:T(8,128)S(1)}, u32[]{:S(2)}, u32[]{:S(2)}) collective-permute-start(f32[1,72,128]{2,1,0:T(8,128)S(1)} %get-tuple-element.18), channel_id=1, source_target_pairs={{0,32},{16,48},{32,0},{48,16},{64,96},{80,112},{96,64},{112,80},{1... | collective-permute-start | bytes 110600 | tf_op jit(solution)/shard_map/ppermute | solution.py:304
  37.6 11.4 %collective-permute-start.2 = (f32[2,72,128]{2,1,0:T(8,128)S(1)}, f32[2,72,128]{2,1,0:T(8,128)S(1)}, u32[]{:S(2)}, u32[]{:S(2)}) collective-permute-start(f32[2,72,128]{2,1,0:T(8,128)S(1)} %pad_maximum_fusion.3), channel_id=1, source_target_pairs={{0,128},{16,144},{32,160},{48,176},{64,192},{80,208},{96,224},{112... | collective-permute-start | bytes 221192 | tf_op jit(solution)/shard_map/ppermute | solution.py:304
  45.5 11.0 %all-to-all-start.1 = ((bf16[16,64,128]{2,1,0:T(8,128)(2,1)}), bf16[16,64,128]{2,1,0:T(8,128)(2,1)S(1)}, u32[]{:S(2)}, u32[]{:S(2)}) async-start(bf16[16,64,128]{2,1,0:T(8,128)(2,1)} %attend.1), calls=%async_computation.1 | async-start | bytes 524288 | tf_op jit(solution)/shard_map/all_to_all | solution.py:328
  49.0 15.6 %collective-permute-start.3 = (f32[4,72,128]{2,1,0:T(8,128)S(1)}, f32[4,72,128]{2,1,0:T(8,128)S(1)}, u32[]{:S(2)}, u32[]{:S(2)}) collective-permute-start(f32[4,72,128]{2,1,0:T(8,128)S(1)} %pad_maximum_fusion.2), channel_id=1, source_target_pairs={{0,64},{16,80},{32,96},{48,112},{64,0},{80,16},{96,32},{112,48},{1... | collective-permute-start | bytes 442376 | tf_op jit(solution)/shard_map/ppermute | solution.py:304
  57.4 18.9 %all-to-all-start.2 = ((bf16[16,64,128]{2,1,0:T(8,128)(2,1)}), bf16[16,64,128]{2,1,0:T(8,128)(2,1)S(1)}, u32[]{:S(2)}, u32[]{:S(2)}) async-start(bf16[16,64,128]{2,1,0:T(8,128)(2,1)} %predict.1), calls=%async_computation.2 | async-start | bytes 524288 | tf_op jit(solution)/shard_map/all_to_all | solution.py:339
  64.6 1.7 %collective-permute-start.4 = (f32[8,72,128]{2,1,0:T(8,128)S(1)}, f32[8,72,128]{2,1,0:T(8,128)S(1)}, u32[]{:S(2)}, u32[]{:S(2)}) collective-permute-start(f32[8,72,128]{2,1,0:T(8,128)S(1)} %pad_maximum_fusion.1), channel_id=1, source_target_pairs={{0,16},{16,0},{32,48},{48,32},{64,80},{80,64},{96,112},{112,96},{1... | collective-permute-start | bytes 884744 | tf_op jit(solution)/shard_map/ppermute | solution.py:304
